TPU v7x, 32 devices: a whole 2x2x4 slice. The times are simulated.
32 devices in a mesh: parts: 2 (over x), rows: 16 (over z, y, core).
Axes of the slice: x: 2, y: 2, z: 4, core: 2. Of those that a mesh axis runs over, the one named last changes fastest.
Arguments:
- gain_tiles: float32 [4, 8192, 3, 128], P(None, ('parts', 'rows')), parts along dimension 1, may hold values from -0.21875 to 0.21875
- tile_pattern: int32 [8, 32, 3], P('parts'), parts along dimension 0, may hold values from 0 to 31, as said below
- offset_terms: float32 [4, 8192], P(None, ('parts', 'rows')), parts along dimension 1, may hold values from -6 to 6
- last_mean: float32 [8192], P(('parts', 'rows')), parts along dimension 0, may hold values from -6 to 6
- last_covariance: float32 [8192, 4096], P(('parts', 'rows')), parts along dimension 0, as said below
- noise_covariance: float32 [4, 8192, 4096], P(None, ('parts', 'rows')), parts along dimension 1, as said below
Outputs:
- smoothed_covariance: float32 [4, 8192, 4096], P(None, ('parts', 'rows')), parts along dimension 1
- smoothed_mean: float32 [4, 8192], P(None, ('parts', 'rows')), parts along dimension 1
There are 2 independent parts, one for each index of `parts`. A program takes and returns all parts, laid end to end along the dimension named above; each array names one. Nothing has to cross between parts.
Inputs may be any that keep to these rules, and one draw needn't show every extreme that they name: `tile_pattern`: each tile row names 3 different tile columns; the first is the tile row's own number. `last_covariance`: symmetric. `noise_covariance`: each block's matrix is symmetric.
All inputs are finite; a program needn't handle non-finite values.
Results may differ from a plain program's by a relative error of at most 0.0001.
Values sent between devices are 32-bit elements; how exact they have to be, the bound alone decides.
A program may use at most 192 MiB of HBM per device.

v0:
```python
import jax
import jax.numpy as jnp
from jax import lax
from jax.sharding import PartitionSpec as P

WIDTH = 4096
TILE = 128
PER_ROW = 3
BLOCKS = 4
TILE_ROWS = 32


def right_product(dense_rows, gain_values, pattern_block):
    row_count = dense_rows.shape[0]
    tiled = dense_rows.reshape(row_count, TILE_ROWS, TILE)
    picked = tiled[:, pattern_block, :]
    shaped = gain_values.reshape(TILE_ROWS, TILE, PER_ROW, TILE)
    result = jnp.einsum("rtkj,tckj->rtc", picked, shaped, precision=lax.Precision.HIGHEST)
    return result.reshape(row_count, WIDTH)


def left_product(columns, gain_values, pattern_block):
    column_count = columns.shape[1]
    tiled = columns.reshape(TILE_ROWS, TILE, column_count)
    picked = tiled[pattern_block]
    shaped = gain_values.reshape(TILE_ROWS, TILE, PER_ROW, TILE)
    result = jnp.einsum("tkjc,tqkj->ctq", picked, shaped, precision=lax.Precision.HIGHEST)
    return result.reshape(column_count, WIDTH)


def shards(gain_tiles, tile_pattern, offset_terms, last_mean, last_covariance, noise_covariance):
    local_rows = last_mean.shape[0]
    first_row = lax.axis_index("rows") * local_rows
    row_numbers = first_row + jnp.arange(local_rows, dtype=jnp.int32)
    tile_match = (
        row_numbers[:, None] // TILE == jnp.arange(TILE_ROWS, dtype=jnp.int32)[None, :]
    ).astype(jnp.int32)
    current_mean = last_mean
    covariance = last_covariance
    cov_list = []
    mean_list = []
    for block_index in reversed(range(BLOCKS)):
        pattern_block = tile_pattern[block_index]
        gain_values = lax.all_gather(gain_tiles[block_index], "rows", axis=0, tiled=True)
        partial_image = right_product(covariance, gain_values, pattern_block)
        received = lax.all_to_all(partial_image, "rows", split_axis=1, concat_axis=0, tiled=True)
        covariance = (
            left_product(received, gain_values, pattern_block) + noise_covariance[block_index]
        )
        cov_list.append(covariance)
        gathered_mean = lax.all_gather(current_mean, "rows", axis=0, tiled=True)
        mean_tiles = gathered_mean.reshape(TILE_ROWS, TILE)
        own_pattern = jnp.sum(tile_match[:, :, None] * pattern_block[None, :, :], axis=1)
        picked = mean_tiles[own_pattern]
        current_mean = (
            jnp.sum(picked * gain_tiles[block_index], axis=(1, 2)) + offset_terms[block_index]
        )
        mean_list.append(current_mean)
    cov_list = cov_list[::-1]
    mean_list = mean_list[::-1]
    return (jnp.stack(cov_list, 0), jnp.stack(mean_list, 0))


def solution(mesh):
    in_specs = (
        P(None, ("parts", "rows"), None, None),
        P("parts", None, None),
        P(None, ("parts", "rows")),
        P(("parts", "rows")),
        P(("parts", "rows"), None),
        P(None, ("parts", "rows"), None),
    )
    out_specs = (P(None, ("parts", "rows"), None), P(None, ("parts", "rows")))
    return jax.shard_map(shards, mesh=mesh, in_specs=in_specs, out_specs=out_specs, check_vma=False)
```

profile of v0, /device:TPU:13, one launch (start us, length us, event | category | flops | bytes accessed | tf_op | source)
XLA Modules:
  0.0 969.5 jit_solution(8600243610957248146)
XLA Ops:
  7.2 2.6 fusion.25
  10.5 5.6 copy.137
  16.1 5.7 copy.139
  22.0 11.3 %gather_fusion = f32[96,256,128]{2,1,0:T(8,128)} fusion(f32[256,32,128]{2,0,1:T(8,128)} %copy.139, s32[1024]{0:T(1024)S(1)} %pad_clamp_fusion.7), kind=kCustom, calls=%fused_computation | custom fusion | bytes 25166208 | tf_op jit(solution)/shard_map/gather | solution.py:16
  33.3 39.4 %all-gather.13.cloned.1.call-done = f32[1,4096,3,128]{3,1,2,0:T(8,128)} async-done(((f32[1,256,3,128]{3,1,2,0:T(8,128)}), f32[1,4096,3,128]{3,1,2,0:T(8,128)}) %all-gather.13.cloned.1.call-update) | async-done | bytes 6291472 | tf_op jit(solution)/shard_map/all_gather | solution.py:44
  72.8 21.4 %fusion.17 = f32[32,256,128,1]{1,2,3,0:T(8,128)} fusion(f32[256,32,3,128]{3,0,2,1:T(8,128)} %bitcast.173, f32[32,128,3,128]{3,1,0,2:T(8,128)} %bitcast.184), kind=kOutput, calls=%fused_computation.30 | convolution fusion | flops 4831838208 | bytes 23068672 | tf_op jit(solution)/shard_map/rtkj,tckj->rtc/dot_general | solution.py:18
  94.2 5.4 copy.141
  99.6 5.7 all-to-all-start
  106.0 9.8 %fusion.24 = (f32[1,256,4096]{2,1,0:T(8,128)}, f32[1,256,4096]{2,1,0:T(8,128)}, f32[1,256,4096]{2,1,0:T(8,128)}) fusion(f32[4,256,4096]{2,1,0:T(8,128)} %param.11), kind=kLoop, calls=%fused_computation.82 | loop fusion | bytes 25165824 | tf_op jit(solution)/shard_map/slice | solution.py:48
  115.8 5.6 copy.143
  121.6 133.8 %all-to-all-done = f32[256,16,256]{2,0,1:T(8,128)} async-done(((f32[256,16,256]{2,0,1:T(8,128)}), f32[256,16,256]{2,0,1:T(8,128)}, u32[]{:S(2)}, u32[]{:S(2)}) %all-to-all-start) | async-done | bytes 4194336 | tf_op jit(solution)/shard_map/all_to_all | solution.py:46
  255.4 11.1 %gather_fusion.1 = f32[96,128,256]{2,1,0:T(8,128)} fusion(f32[32,128,256]{2,1,0:T(8,128)} %bitcast.10, s32[1024]{0:T(1024)S(1)} %pad_clamp_fusion.7), kind=kCustom, calls=%fused_computation.1 | custom fusion | bytes 25166208 | tf_op jit(solution)/shard_map/gather | solution.py:25
  266.5 15.3 %bitcast_add_fusion = (f32[256,32,128]{0,2,1:T(8,128)}, f32[32,256,128,1]{1,2,3,0:T(8,128)}) fusion(f32[256,32,128]{0,2,1:T(8,128)} %bitcast.190, f32[32,3,128,256]{3,2,1,0:T(8,128)} %bitcast.174, f32[32,128,3,128]{3,1,0,2:T(8,128)} %bitcast.185), kind=kOutput, calls=%fused_computation.32 | convolution fusion | flops 4832886784 | bytes 31457280 | tf_op jit(solution)/shard_map/tkjc,tqkj->ctq/dot_general | solution.py:27
  281.9 11.1 %gather_fusion.2 = f32[96,256,128]{1,2,0:T(8,128)} fusion(f32[256,32,128]{0,2,1:T(8,128)} %get-tuple-element.32, s32[1024]{0:T(1024)S(1)} %pad_clamp_fusion.6), kind=kCustom, calls=%fused_computation.2 | custom fusion | bytes 25166208 | tf_op jit(solution)/shard_map/gather | solution.py:16
  292.9 12.7 %copy.145 = f32[32,3,256,128]{3,2,1,0:T(8,128)} copy(f32[32,3,256,128]{2,3,1,0:T(8,128)} %bitcast.170) | data formatting | bytes 25165824 | tf_op jit(solution)/shard_map/gather | solution.py:16
  305.7 21.4 %fusion.4 = f32[32,256,128,1]{1,2,3,0:T(8,128)} fusion(f32[32,3,256,128]{3,2,1,0:T(8,128)} %copy.145, f32[32,128,3,128]{3,1,0,2:T(8,128)} %bitcast.182), kind=kOutput, calls=%fused_computation.17 | convolution fusion | flops 4831838208 | bytes 23068672 | tf_op jit(solution)/shard_map/rtkj,tckj->rtc/dot_general | solution.py:18
  327.1 5.4 copy.147
  332.5 4.5 all-to-all-start.1
  337.5 5.8 copy.149
  343.6 123.4 %all-to-all-done.1 = f32[256,16,256]{2,0,1:T(8,128)} async-done(((f32[256,16,256]{2,0,1:T(8,128)}), f32[256,16,256]{2,0,1:T(8,128)}, u32[]{:S(2)}, u32[]{:S(2)}) %all-to-all-start.1) | async-done | bytes 4194336 | tf_op jit(solution)/shard_map/all_to_all | solution.py:46
  467.0 11.1 %gather_fusion.3 = f32[96,128,256]{2,1,0:T(8,128)} fusion(f32[32,128,256]{2,1,0:T(8,128)} %bitcast.25, s32[1024]{0:T(1024)S(1)} %pad_clamp_fusion.6), kind=kCustom, calls=%fused_computation.3 | custom fusion | bytes 25166208 | tf_op jit(solution)/shard_map/gather | solution.py:25
  478.1 15.3 %bitcast_add_fusion.1 = (f32[256,32,128]{0,2,1:T(8,128)}, f32[32,256,128,1]{1,2,3,0:T(8,128)}) fusion(f32[256,32,128]{0,2,1:T(8,128)} %bitcast.191, f32[32,3,128,256]{3,2,1,0:T(8,128)} %bitcast.175, f32[32,128,3,128]{3,1,0,2:T(8,128)} %bitcast.183), kind=kOutput, calls=%fused_computation.33 | convolution fusion | flops 4832886784 | bytes 31457280 | tf_op jit(solution)/shard_map/tkjc,tqkj->ctq/dot_general | solution.py:27
  493.4 11.1 %gather_fusion.4 = f32[96,256,128]{1,2,0:T(8,128)} fusion(f32[256,32,128]{0,2,1:T(8,128)} %get-tuple-element.34, s32[1024]{0:T(1024)S(1)} %pad_clamp_fusion.5), kind=kCustom, calls=%fused_computation.4 | custom fusion | bytes 25166208 | tf_op jit(solution)/shard_map/gather | solution.py:16
  504.5 13.0 %copy.151 = f32[32,3,256,128]{3,2,1,0:T(8,128)} copy(f32[32,3,256,128]{2,3,1,0:T(8,128)} %bitcast.171) | data formatting | bytes 25165824 | tf_op jit(solution)/shard_map/gather | solution.py:16
  517.5 21.4 %fusion.2 = f32[32,256,128,1]{1,2,3,0:T(8,128)} fusion(f32[32,3,256,128]{3,2,1,0:T(8,128)} %copy.151, f32[32,128,3,128]{3,1,0,2:T(8,128)} %bitcast.180), kind=kOutput, calls=%fused_computation.15 | convolution fusion | flops 4831838208 | bytes 23068672 | tf_op jit(solution)/shard_map/rtkj,tckj->rtc/dot_general | solution.py:18
  538.9 5.4 copy.153
  544.3 5.2 all-to-all-start.2
  549.5 5.6 copy.155
  555.3 86.5 %all-to-all-done.2 = f32[256,16,256]{2,0,1:T(8,128)} async-done(((f32[256,16,256]{2,0,1:T(8,128)}), f32[256,16,256]{2,0,1:T(8,128)}, u32[]{:S(2)}, u32[]{:S(2)}) %all-to-all-start.2) | async-done | bytes 4194336 | tf_op jit(solution)/shard_map/all_to_all | solution.py:46
  641.8 11.1 %gather_fusion.5 = f32[96,128,256]{2,1,0:T(8,128)} fusion(f32[32,128,256]{2,1,0:T(8,128)} %bitcast.40, s32[1024]{0:T(1024)S(1)} %pad_clamp_fusion.5), kind=kCustom, calls=%fused_computation.5 | custom fusion | bytes 25166208 | tf_op jit(solution)/shard_map/gather | solution.py:25
  652.9 15.2 %bitcast_add_fusion.2 = (f32[256,32,128]{0,2,1:T(8,128)}, f32[32,256,128,1]{1,2,3,0:T(8,128)}) fusion(f32[256,32,128]{0,2,1:T(8,128)} %bitcast.189, f32[32,3,128,256]{3,2,1,0:T(8,128)} %bitcast.176, f32[32,128,3,128]{3,1,0,2:T(8,128)} %bitcast.181), kind=kOutput, calls=%fused_computation.34 | convolution fusion | flops 4832886784 | bytes 31457280 | tf_op jit(solution)/shard_map/tkjc,tqkj->ctq/dot_general | solution.py:27
  668.1 11.1 %gather_fusion.6 = f32[96,256,128]{1,2,0:T(8,128)} fusion(f32[256,32,128]{0,2,1:T(8,128)} %get-tuple-element.36, s32[1024]{0:T(1024)S(1)} %pad_clamp_fusion.4), kind=kCustom, calls=%fused_computation.6 | custom fusion | bytes 25166208 | tf_op jit(solution)/shard_map/gather | solution.py:16
  679.2 12.8 %copy.157 = f32[32,3,256,128]{3,2,1,0:T(8,128)} copy(f32[32,3,256,128]{2,3,1,0:T(8,128)} %bitcast.172) | data formatting | bytes 25165824 | tf_op jit(solution)/shard_map/gather | solution.py:16
  692.0 21.4 %fusion = f32[32,256,128,1]{1,2,3,0:T(8,128)} fusion(f32[32,3,256,128]{3,2,1,0:T(8,128)} %copy.157, f32[32,128,3,128]{3,1,0,2:T(8,128)} %bitcast.178), kind=kOutput, calls=%fused_computation.13 | convolution fusion | flops 4831838208 | bytes 23068672 | tf_op jit(solution)/shard_map/rtkj,tckj->rtc/dot_general | solution.py:18
  713.4 5.3 copy.159
  718.8 5.4 all-to-all-start.3
  724.8 101.0 %all-gather.4 = f32[16,1,256]{2,1,0:T(1,128)S(1)} all-gather(f32[1,1,256]{2,1,0:T(1,128)S(1)} %bitcast.208), channel_id=1, replica_groups=mesh['parts'=2,'rows'=16] {'rows'}, dimensions={0}, use_global_device_ids=true | all-gather | bytes 17408 | tf_op jit(solution)/shard_map/all_gather | solution.py:51
  828.2 15.0 %all-gather.5 = f32[16,1,256]{2,1,0:T(1,128)S(1)} all-gather(f32[1,1,256]{2,1,0:T(1,128)S(1)} %bitcast.201), channel_id=1, replica_groups=mesh['parts'=2,'rows'=16] {'rows'}, dimensions={0}, use_global_device_ids=true | all-gather | bytes 17408 | tf_op jit(solution)/shard_map/all_gather | solution.py:51
  845.4 20.3 %all-gather.6 = f32[16,1,256]{2,1,0:T(1,128)S(1)} all-gather(f32[1,1,256]{2,1,0:T(1,128)S(1)} %bitcast.202), channel_id=1, replica_groups=mesh['parts'=2,'rows'=16] {'rows'}, dimensions={0}, use_global_device_ids=true | all-gather | bytes 17408 | tf_op jit(solution)/shard_map/all_gather | solution.py:51
  868.0 17.4 %all-gather.7 = f32[16,1,256]{2,1,0:T(1,128)S(1)} all-gather(f32[1,1,256]{2,1,0:T(1,128)S(1)} %bitcast.203), channel_id=1, replica_groups=mesh['parts'=2,'rows'=16] {'rows'}, dimensions={0}, use_global_device_ids=true | all-gather | bytes 17408 | tf_op jit(solution)/shard_map/all_gather | solution.py:51
  887.9 5.7 copy.164
  893.6 5.7 copy.163
  899.2 5.6 copy.162
  904.9 11.1 %gather_fusion.7 = f32[96,128,256]{2,1,0:T(8,128)} fusion(f32[32,128,256]{2,1,0:T(8,128)} %bitcast.55, s32[1024]{0:T(1024)S(1)} %pad_clamp_fusion.4), kind=kCustom, calls=%fused_computation.7 | custom fusion | bytes 25166208 | tf_op jit(solution)/shard_map/gather | solution.py:25
  916.0 14.0 %fusion.6 = f32[32,256,128,1]{1,2,3,0:T(8,128)} fusion(f32[32,3,128,256]{3,2,1,0:T(8,128)} %bitcast.177, f32[32,128,3,128]{3,1,0,2:T(8,128)} %bitcast.179), kind=kOutput, calls=%fused_computation.19 | convolution fusion | flops 4831838208 | bytes 23068672 | tf_op jit(solution)/shard_map/tkjc,tqkj->ctq/dot_general | solution.py:27
  929.9 5.6 copy.161
  935.5 16.2 %slice_add_fusion = (f32[1,256,4096]{2,1,0:T(8,128)S(1)}, f32[1,256,4096]{2,1,0:T(8,128)}, f32[1,256,4096]{2,1,0:T(8,128)}, f32[1,256,4096]{2,1,0:T(8,128)}) fusion(f32[1,256,4096]{2,1,0:T(8,128)} %copy.161, f32[4,256,4096]{2,1,0:T(8,128)} %param.11, f32[1,256,4096]{2,1,0:T(8,128)} %copy.164, f32[1,256,4096]{2,1,0:T(8,128)} %copy.163, f32[1,256,4096]{2,1,0:T(8,128)} %copy.162), kind=kLoop, calls=%fused_computation.35 | loop fusion | flops 4194304 | bytes 50331648 | tf_op jit(solution)/shard_map/add | solution.py:48
  951.8 10.7 %pad_maximum_fusion = f32[4,256,4096]{2,1,0:T(8,128)} fusion(f32[1,256,4096]{2,1,0:T(8,128)} %get-tuple-element.7, f32[1,256,4096]{2,1,0:T(8,128)} %get-tuple-element.8, f32[1,256,4096]{2,1,0:T(8,128)} %get-tuple-element.9, f32[1,256,4096]{2,1,0:T(8,128)S(1)} %get-tuple-element.6), kind=kLoop, calls=%fused_computation.12 | loop fusion | flops 12582912 | bytes 33554432 | tf_op jit(solution)/shard_map/stack | solution.py:61
  (75 shorter events, 12.6 us)
Async XLA Ops:
  7.2 65.6 %all-gather.13.cloned.1.call-start = ((), (), s32[]{:S(2)}) async-start(), calls=%async_computation.4 | async-start | bytes 6684672 | tf_op jit(solution)/shard_map/all_gather | solution.py:44
  9.8 295.9 %all-gather.15.cloned.1.call-start = ((), (), s32[]{:S(2)}) async-start(), calls=%async_computation.5 | async-start | bytes 6684672 | tf_op jit(solution)/shard_map/all_gather | solution.py:44
  16.1 5.7 copy-start.1
  99.6 155.8 %all-to-all-start = ((f32[256,16,256]{2,0,1:T(8,128)}), f32[256,16,256]{2,0,1:T(8,128)}, u32[]{:S(2)}, u32[]{:S(2)}) async-start(f32[256,16,256]{2,0,1:T(8,128)} %copy.141), calls=%async_computation | async-start | bytes 8388608 | tf_op jit(solution)/shard_map/all_to_all | solution.py:46
  105.2 412.2 %all-gather.17.cloned.1.call-start = ((), (), s32[]{:S(2)}) async-start(), calls=%async_computation.6 | async-start | bytes 6684672 | tf_op jit(solution)/shard_map/all_gather | solution.py:44
  332.5 134.5 %all-to-all-start.1 = ((f32[256,16,256]{2,0,1:T(8,128)}), f32[256,16,256]{2,0,1:T(8,128)}, u32[]{:S(2)}, u32[]{:S(2)}) async-start(f32[256,16,256]{2,0,1:T(8,128)} %copy.147), calls=%async_computation.1 | async-start | bytes 8388608 | tf_op jit(solution)/shard_map/all_to_all | solution.py:46
  337.0 355.0 %all-gather.19.cloned.1.call-start = ((), (), s32[]{:S(2)}) async-start(), calls=%async_computation.7 | async-start | bytes 6684672 | tf_op jit(solution)/shard_map/all_gather | solution.py:44
  544.3 97.6 %all-to-all-start.2 = ((f32[256,16,256]{2,0,1:T(8,128)}), f32[256,16,256]{2,0,1:T(8,128)}, u32[]{:S(2)}, u32[]{:S(2)}) async-start(f32[256,16,256]{2,0,1:T(8,128)} %copy.153), calls=%async_computation.2 | async-start | bytes 8388608 | tf_op jit(solution)/shard_map/all_to_all | solution.py:46
  718.8 5.5 copy-start.2
  718.8 6.1 copy-start.4
  718.8 109.2 %copy-start = (f32[4,256,3,128]{3,1,2,0:T(8,128)S(1)}, f32[4,256,3,128]{3,1,2,0:T(8,128)}, u32[]{:S(2)}) copy-start(f32[4,256,3,128]{3,1,2,0:T(8,128)} %param.6) | copy-start | bytes 4718596
  718.8 109.4 %copy-start.3 = (f32[4,256]{1,0:T(4,128)S(1)}, f32[4,256]{1,0:T(4,128)}, u32[]{:S(2)}) copy-start(f32[4,256]{1,0:T(4,128)} %param.8) | copy-start | bytes 12292
  718.8 186.1 %all-to-all-start.3 = ((f32[256,16,256]{2,0,1:T(8,128)}), f32[256,16,256]{2,0,1:T(8,128)}, u32[]{:S(2)}, u32[]{:S(2)}) async-start(f32[256,16,256]{2,0,1:T(8,128)} %copy.159), calls=%async_computation.3 | async-start | bytes 8388608 | tf_op jit(solution)/shard_map/all_to_all | solution.py:46
Sparse Core Ops, SparseCore 0:
  10.2 62.5 all-gather.12
  74.9 99.0 all-gather.14
  176.2 82.8 all-gather.16
  339.7 110.3 all-gather.18
where the time goes:
time: 979 us; the launch traced here: 969 us
  waiting for transfers between devices  385 us (39%)
  local copies, waits for them, and re-layouts  221 us (23%)
  blocking collectives  154 us (16%)
  matrix products  145 us (15%)
  other arithmetic  28.3 us (3%)
  starting transfers between devices  21.3 us (2%)
  between operations  14.6 us (1%)
    all_to_all x4, waiting for transfers between devices, shards(): lax.all_to_all(partial_image, 'rows', split_axis=1, concat_axis=0, tiled=...  344 us
    all_gather x4, blocking collectives, shards(): gathered_mean = lax.all_gather(current_mean, 'rows', axis=0, tiled=True)  154 us
    dot_general x4, matrix products, right_product(): jnp.einsum('rtkj,tckj->rtc', picked, shaped, precision=lax.Precision.HIGH...  85.7 us
    gather x7, local copies, waits for them, and re-layouts, right_product(): picked = tiled[:, pattern_block, :]  83 us
    dot_general x4, matrix products, left_product(): jnp.einsum('tkjc,tqkj->ctq', picked, shaped, precision=lax.Precision.HIGH...  59.8 us
    gather x4, local copies, waits for them, and re-layouts, left_product(): picked = tiled[pattern_block]  44.4 us
    all_gather x4, waiting for transfers between devices, shards(): lax.all_gather(gain_tiles[block_index], 'rows', axis=0, tiled=True)  39.5 us
    slice x4, local copies, waits for them, and re-layouts, shards(): noise_covariance[block_index]  26.9 us
  transfers between devices with their start and end apart: 8, of which 4 were waited for; matrix products, arithmetic and copies ran while one was open for 32% of the time, Pallas kernels for 0%

commit v1 on v0

v1 whole, which is shorter than its diff:
```python
import functools

import jax
import jax.numpy as jnp
from jax import lax
from jax.experimental import pallas as pl
from jax.experimental.pallas import tpu as pltpu
from jax.sharding import PartitionSpec as P

WIDTH = 4096
TILE = 128
PER_ROW = 3
BLOCKS = 4
TILE_ROWS = 32
STEP = 512
STEPS = WIDTH // STEP
PAD = 16
VMEM = 56 * 1024 * 1024


def split(x):
    high = x.astype(jnp.bfloat16)
    low = (x - high.astype(jnp.float32)).astype(jnp.bfloat16)
    return high, low


def nt(a, b):
    return lax.dot_general(a, b, (((1,), (1,)), ((), ())), preferred_element_type=jnp.float32)


def product(ah, al, bh, bl):
    return nt(ah, bh) + (nt(ah, bl) + nt(al, bh))


def gain_parts(gain_ref):
    parts = [gain_ref[:, k].reshape(STEP, TILE) for k in range(PER_ROW)]
    return split(jnp.concatenate(parts, axis=1))


def picked(ref, pattern_ref, block, tile):
    at = (block * TILE_ROWS + tile) * PER_ROW
    return jnp.concatenate([ref[pattern_ref[at + k]] for k in range(PER_ROW)], axis=1)


def right_kernel(block, pattern_ref, cov_ref, gain_ref, send_ref, high, low):
    step = pl.program_id(0)

    @pl.when(step == 0)
    def _():
        for p in range(TILE_ROWS):
            high[p], low[p] = split(cov_ref[:, p * TILE:(p + 1) * TILE])

    gh, gl = gain_parts(gain_ref)
    local = cov_ref.shape[0]
    rows = []
    for i in range(STEP // TILE):
        tile = step * (STEP // TILE) + i
        ph, pw = picked(high, pattern_ref, block, tile), picked(low, pattern_ref, block, tile)
        s = slice(i * TILE, (i + 1) * TILE)
        rows.append(product(gh[s], gl[s], ph, pw))
    send_ref[...] = jnp.concatenate(rows, axis=0).reshape(STEP // local, local, local)


def left_kernel(block, pattern_ref, recv_ref, gain_ref, noise_ref, mean_ref, offset_ref, *rest):
    cov_ref, new_mean_ref, high, low = rest[-4:]
    step = pl.program_id(0)
    local = recv_ref.shape[1]

    @pl.when(step == 0)
    def _():
        for p in range(TILE_ROWS):
            if local >= TILE:
                per = local // TILE
                x = recv_ref[p // per, :, (p % per) * TILE:(p % per + 1) * TILE]
            else:
                per = TILE // local
                x = jnp.concatenate([recv_ref[p * per + i] for i in range(per)], axis=1)
            high[p, :local], low[p, :local] = split(x)
            m = jnp.broadcast_to(mean_ref[p], (PAD, TILE))
            high[p, local:], low[p, local:] = split(m)

    gh, gl = gain_parts(gain_ref)
    for i in range(STEP // TILE):
        tile = step * (STEP // TILE) + i
        xh, xl = picked(high, pattern_ref, block, tile), picked(low, pattern_ref, block, tile)
        s = slice(i * TILE, (i + 1) * TILE)
        out = product(xh, xl, gh[s], gl[s])
        cov_ref[:, s] = out[:local] + noise_ref[:, s]
        new_mean_ref[i] = out[local:local + 1] + offset_ref[i]


def right(block, pattern, cov, cov_at, gain, n, local):
    if cov_at is None:
        cov_spec = pl.BlockSpec((local, WIDTH), lambda i, s: (0, 0))
    else:
        cov_spec = pl.BlockSpec((None, local, WIDTH), lambda i, s: (cov_at, 0, 0))
    per = STEP // local
    return pl.pallas_call(
        functools.partial(right_kernel, block),
        out_shape=jax.ShapeDtypeStruct((n, local, local), jnp.float32),
        grid_spec=pltpu.PrefetchScalarGridSpec(
            num_scalar_prefetch=1,
            grid=(STEPS,),
            in_specs=[
                cov_spec,
                pl.BlockSpec((per, PER_ROW, local, TILE), lambda i, s: (i, 0, 0, 0)),
            ],
            out_specs=pl.BlockSpec((per, local, local), lambda i, s: (i, 0, 0)),
            scratch_shapes=[pltpu.VMEM((TILE_ROWS, local, TILE), jnp.bfloat16)] * 2,
        ),
        compiler_params=pltpu.CompilerParams(vmem_limit_bytes=VMEM),
        name="right_product",
    )(pattern, cov, gain)


def left(block, pattern, recv, gain, noise, mean, offset, stack, n, local):
    per = STEP // local
    tiles = STEP // TILE
    in_specs = [
        pl.BlockSpec((n, local, local), lambda i, s: (0, 0, 0)),
        pl.BlockSpec((per, PER_ROW, local, TILE), lambda i, s: (i, 0, 0, 0)),
        pl.BlockSpec((None, local, STEP), lambda i, s: (block, 0, i)),
        pl.BlockSpec((TILE_ROWS, 1, TILE), lambda i, s: (0, 0, 0)),
        pl.BlockSpec((tiles, 1, TILE), lambda i, s: (i, 0, 0)),
    ]
    args = [pattern, recv, gain, noise, mean, offset]
    aliases = {}
    if stack is not None:
        in_specs.append(pl.BlockSpec(memory_space=pl.ANY))
        args.append(stack)
        aliases = {6: 0}
    return pl.pallas_call(
        functools.partial(left_kernel, block),
        out_shape=(
            jax.ShapeDtypeStruct((BLOCKS, local, WIDTH), jnp.float32),
            jax.ShapeDtypeStruct((TILE_ROWS, 1, TILE), jnp.float32),
        ),
        grid_spec=pltpu.PrefetchScalarGridSpec(
            num_scalar_prefetch=1,
            grid=(STEPS,),
            in_specs=in_specs,
            out_specs=(
                pl.BlockSpec((None, local, STEP), lambda i, s: (block, 0, i)),
                pl.BlockSpec((tiles, 1, TILE), lambda i, s: (i, 0, 0)),
            ),
            scratch_shapes=[pltpu.VMEM((TILE_ROWS, local + PAD, TILE), jnp.bfloat16)] * 2,
        ),
        input_output_aliases=aliases,
        compiler_params=pltpu.CompilerParams(vmem_limit_bytes=VMEM),
        name="left_product",
    )(*args)


def shards(n, gain_tiles, tile_pattern, offset_terms, last_mean, last_covariance, noise_covariance):
    local = last_mean.shape[0]
    pattern = tile_pattern.reshape(-1)
    gains = jnp.transpose(gain_tiles, (0, 2, 1, 3))
    gathered = {b: lax.all_gather(gains[b], "rows") for b in reversed(range(BLOCKS))}
    vectors = lax.all_gather(jnp.concatenate([offset_terms, last_mean[None]], 0), "rows")
    vectors = jnp.transpose(vectors, (1, 0, 2)).reshape(BLOCKS + 1, TILE_ROWS, 1, TILE)
    mean = vectors[BLOCKS]
    stack = None
    means = [None] * BLOCKS
    for b in reversed(range(BLOCKS)):
        if stack is None:
            send = right(b, pattern, last_covariance, None, gathered[b], n, local)
        else:
            send = right(b, pattern, stack, b + 1, gathered[b], n, local)
        recv = lax.all_to_all(send, "rows", split_axis=0, concat_axis=0, tiled=True)
        stack, mean = left(
            b, pattern, recv, gathered[b], noise_covariance, mean, vectors[b], stack, n, local
        )
        means[b] = mean.reshape(WIDTH)
    first = lax.axis_index("rows") * local
    own = lax.dynamic_slice(jnp.stack(means, 0), (0, first), (BLOCKS, local))
    return stack, own


def solution(mesh):
    in_specs = (
        P(None, ("parts", "rows"), None, None),
        P("parts", None, None),
        P(None, ("parts", "rows")),
        P(("parts", "rows")),
        P(("parts", "rows"), None),
        P(None, ("parts", "rows"), None),
    )
    out_specs = (P(None, ("parts", "rows"), None), P(None, ("parts", "rows")))
    return jax.shard_map(
        functools.partial(shards, mesh.shape["rows"]),
        mesh=mesh, in_specs=in_specs, out_specs=out_specs, check_vma=False,
    )
```

time: 979 us -> 675 us (0.69)
  local copies, waits for them, and re-layouts: 221 us -> 4.79 us
  matrix products: 145 us -> 0 us
  Pallas kernels: 0 us -> 111 us
  waiting for transfers between devices: 385 us -> 286 us
  blocking collectives: 154 us -> 238 us
  other arithmetic: 28.3 us -> 1.31 us
    dot_general x8 -> x0, matrix products: 145 us -> none  [the longest x4 85.7 us: right_product(): jnp.einsum('rtkj,tckj->rtc', picked, shaped, precision=lax.Precision.HIGH...]
    gather x19 -> x0, local copies, waits for them, and re-layouts: 134 us -> none  [the longest x7 83 us: right_product(): picked = tiled[:, pattern_block, :]]
    all_to_all x4 -> x3, waiting for transfers between devices: 344 us -> 223 us  [shards(): recv = lax.all_to_all(send, 'rows', split_axis=0, concat_axis=0, tiled=True)]
    pallas_call x0 -> x8, Pallas kernels: none -> 111 us  [the longest x4 59.2 us: left(): pl.pallas_call(functools.partial(left_kernel, block), out_shape=(jax.Shap...]
    all_to_all x0 -> x1, blocking collectives: none -> 96.9 us  [shards(): recv = lax.all_to_all(send, 'rows', split_axis=0, concat_axis=0, tiled=True)]
    reshape x5 -> x1, local copies, waits for them, and re-layouts: 28.2 us -> 0.79 us  [shards(): pattern = tile_pattern.reshape(-1)]
    slice x7 -> x2, local copies, waits for them, and re-layouts: 29.5 us -> 3.19 us  [the longest x1 2.51 us: shards(): gains[b]]
    all_gather x4, waiting for transfers between devices: 39.5 us -> 61.3 us  [shards(): lax.all_gather(gains[b], 'rows')]
  transfers between devices with their start and end apart: 8 -> 7, of which waited for: 4 -> 3; matrix products, arithmetic and copies ran while one was open for 32% -> 0% of each run, Pallas kernels for 0% -> 12%
where the time goes in v1:
time: 675 us; the launch traced here: 673 us
  waiting for transfers between devices  286 us (42%)
  blocking collectives  238 us (35%)
  Pallas kernels  111 us (16%)
  starting transfers between devices  17.7 us (3%)
  between operations  13.8 us (2%)
    all_to_all x3, waiting for transfers between devices, shards(): recv = lax.all_to_all(send, 'rows', split_axis=0, concat_axis=0, tiled=True)  223 us
    all_gather x1, blocking collectives, shards(): lax.all_gather(jnp.concatenate([offset_terms, last_mean[None]], 0), 'rows')  141 us
    all_to_all x1, blocking collectives, shards(): recv = lax.all_to_all(send, 'rows', split_axis=0, concat_axis=0, tiled=True)  96.9 us
    all_gather x4, waiting for transfers between devices, shards(): lax.all_gather(gains[b], 'rows')  61.3 us
    pallas_call x4, Pallas kernels, left(): pl.pallas_call(functools.partial(left_kernel, block), out_shape=(jax.Shap...  59.2 us
    pallas_call x4, Pallas kernels, right(): pl.pallas_call(functools.partial(right_kernel, block), out_shape=jax.Shap...  52.2 us
    all_to_all x3, starting transfers between devices, shards(): recv = lax.all_to_all(send, 'rows', split_axis=0, concat_axis=0, tiled=True)  17.6 us
  transfers between devices with their start and end apart: 7, of which 3 were waited for; matrix products, arithmetic and copies ran while one was open for 0% of the time, Pallas kernels for 12%

profile of v1, /device:TPU:13, one launch (start us, length us, event | category | flops | bytes accessed | tf_op | source)
XLA Modules:
  0.0 672.8 jit_solution(8844810728077750383)
XLA Ops:
  7.2 0.0 all-gather.7.cloned.1.call-start
  7.2 2.5 fusion.3
  9.7 0.0 all-gather.7.cloned.1.call-update
  9.7 0.0 all-gather.9.cloned.1.call-start
  9.8 0.7 all-gather.9.cloned.1.call-update
  10.5 0.8 copy.12
  11.3 0.8 reshape.18.pattern_ref
  12.1 61.3 %all-gather.7.cloned.1.call-done.gain_ref = f32[16,3,256,128]{3,2,1,0:T(8,128)} async-done(((f32[1,3,256,128]{3,2,1,0:T(8,128)}), f32[16,3,256,128]{3,2,1,0:T(8,128)}) %all-gather.7.cloned.1.call-update) | async-done | bytes 6291472 | tf_op jit(solution)/shard_map/all_gather | solution.py:158
  73.3 13.0 %right_product.4 = f32[16,256,256]{2,1,0:T(8,128)} custom-call(s32[384]{0:T(512)} %reshape.18.pattern_ref, f32[256,4096]{1,0:T(8,128)} %cov_ref.1, f32[16,3,256,128]{3,2,1,0:T(8,128)} %all-gather.7.cloned.1.call-done.gain_ref), custom_call_target="tpu_custom_call" | custom-call | tf_op jit(solution)/shard_map/right_product/pallas_call | solution.py:98
  86.3 0.0 copy-start.3
  86.3 0.0 copy-start.4
  86.3 5.8 all-to-all-start
  92.1 0.0 all-gather.11.cloned.1.call-start
  92.1 0.7 all-gather.11.cloned.1.call-update
  92.8 0.0 copy-done.3
  92.8 0.0 copy-done.4
  92.9 141.1 %all-gather.1 = f32[16,5,256]{2,1,0:T(8,128)S(1)} all-gather(f32[1,5,256]{2,1,0:T(8,128)S(1)} %maximum_bitcast_fusion), channel_id=2, replica_groups=mesh['parts'=2,'rows'=16] {'rows'}, dimensions={0}, use_global_device_ids=true | all-gather | bytes 87040 | tf_op jit(solution)/shard_map/all_gather | solution.py:159
  234.0 0.7 fusion.4
  234.7 0.0 all-to-all-done.recv_ref
  234.7 14.9 %left_product.4 = (f32[4,256,4096]{2,1,0:T(8,128)}, f32[32,1,128]{2,1,0:T(1,128)}) custom-call(s32[384]{0:T(512)} %reshape.18.pattern_ref, f32[16,256,256]{2,1,0:T(8,128)} %all-to-all-done.recv_ref, f32[16,3,256,128]{3,2,1,0:T(8,128)} %all-gather.7.cloned.1.call-done.gain_ref, f32[4,256,4096]{2,1,0:T(8,128)} %noise_ref.7, f32[32,1,128]{2,1,0:T(1,128)} %bitcast.23, ...), custom_call_target="tpu_custom_call" | custom-call | tf_op jit(solution)/shard_map/left_product/pallas_call | solution.py:132
  249.5 0.0 all-gather.9.cloned.1.call-done.gain_ref
  249.5 13.2 %right_product.5 = f32[16,256,256]{2,1,0:T(8,128)} custom-call(s32[384]{0:T(512)} %reshape.18.pattern_ref, f32[4,256,4096]{2,1,0:T(8,128)} %get-tuple-element.10.cov_ref.rest_0_, f32[16,3,256,128]{3,2,1,0:T(8,128)} %all-gather.9.cloned.1.call-done.gain_ref), custom_call_target="tpu_custom_call" | custom-call | tf_op jit(solution)/shard_map/right_product/pallas_call | solution.py:98
  262.8 6.5 all-to-all-start.1
  269.3 0.0 all-gather.13.cloned.1.call-start
  269.3 0.5 all-gather.13.cloned.1.call-update
  269.8 130.2 %all-to-all-done.1.recv_ref = f32[16,256,256]{2,1,0:T(8,128)} async-done(((f32[16,256,256]{2,1,0:T(8,128)}), f32[16,256,256]{2,1,0:T(8,128)}, u32[]{:S(2)}, u32[]{:S(2)}) %all-to-all-start.1) | async-done | bytes 4194336 | tf_op jit(solution)/shard_map/all_to_all | solution.py:169
  400.0 14.7 %left_product.5 = (f32[4,256,4096]{2,1,0:T(8,128)}, f32[32,1,128]{2,1,0:T(1,128)}) custom-call(s32[384]{0:T(512)} %reshape.18.pattern_ref, f32[16,256,256]{2,1,0:T(8,128)} %all-to-all-done.1.recv_ref, f32[16,3,256,128]{3,2,1,0:T(8,128)} %all-gather.9.cloned.1.call-done.gain_ref, f32[4,256,4096]{2,1,0:T(8,128)} %noise_ref.7, ...), custom_call_target="tpu_custom_call", output_to_operand_aliasing={{0}: (6, {})} | custom-call | tf_op jit(solution)/shard_map/left_product/pallas_call | solution.py:132
  414.7 0.0 all-gather.11.cloned.1.call-done.gain_ref
  414.7 12.9 %right_product.6 = f32[16,256,256]{2,1,0:T(8,128)} custom-call(s32[384]{0:T(512)} %reshape.18.pattern_ref, f32[4,256,4096]{2,1,0:T(8,128)} %get-tuple-element.12.cov_ref.rest_0_, f32[16,3,256,128]{3,2,1,0:T(8,128)} %all-gather.11.cloned.1.call-done.gain_ref), custom_call_target="tpu_custom_call" | custom-call | tf_op jit(solution)/shard_map/right_product/pallas_call | solution.py:98
  427.7 96.9 %all_to_all.20.recv_ref = f32[16,256,256]{2,1,0:T(8,128)} all-to-all(f32[16,256,256]{2,1,0:T(8,128)} %right_product.6), channel_id=1, replica_groups=mesh['parts'=2,'rows'=16] {'rows'}, dimensions={0} | all-to-all | bytes 8388608 | tf_op jit(solution)/shard_map/all_to_all | solution.py:169
  524.6 14.7 %left_product.6 = (f32[4,256,4096]{2,1,0:T(8,128)}, f32[32,1,128]{2,1,0:T(1,128)}) custom-call(s32[384]{0:T(512)} %reshape.18.pattern_ref, f32[16,256,256]{2,1,0:T(8,128)} %all_to_all.20.recv_ref, f32[16,3,256,128]{3,2,1,0:T(8,128)} %all-gather.11.cloned.1.call-done.gain_ref, f32[4,256,4096]{2,1,0:T(8,128)} %noise_ref.7, ...), custom_call_target="tpu_custom_call", output_to_operand_aliasing={{0}: (6, {})} | custom-call | tf_op jit(solution)/shard_map/left_product/pallas_call | solution.py:132
  539.3 0.0 all-gather.13.cloned.1.call-done.gain_ref
  539.3 13.0 %right_product.7 = f32[16,256,256]{2,1,0:T(8,128)} custom-call(s32[384]{0:T(512)} %reshape.18.pattern_ref, f32[4,256,4096]{2,1,0:T(8,128)} %get-tuple-element.14.cov_ref.rest_0_, f32[16,3,256,128]{3,2,1,0:T(8,128)} %all-gather.13.cloned.1.call-done.gain_ref), custom_call_target="tpu_custom_call" | custom-call | tf_op jit(solution)/shard_map/right_product/pallas_call | solution.py:98
  552.3 5.3 all-to-all-start.3
  557.6 92.5 %all-to-all-done.3.recv_ref = f32[16,256,256]{2,1,0:T(8,128)} async-done(((f32[16,256,256]{2,1,0:T(8,128)}), f32[16,256,256]{2,1,0:T(8,128)}, u32[]{:S(2)}, u32[]{:S(2)}) %all-to-all-start.3) | async-done | bytes 4194336 | tf_op jit(solution)/shard_map/all_to_all | solution.py:169
  650.1 0.0 copy-start
  650.1 0.0 copy-start.1
  650.1 0.0 copy-start.2
  650.1 14.9 %left_product.7 = (f32[4,256,4096]{2,1,0:T(8,128)}, f32[32,1,128]{2,1,0:T(1,128)}) custom-call(s32[384]{0:T(512)} %reshape.18.pattern_ref, f32[16,256,256]{2,1,0:T(8,128)} %all-to-all-done.3.recv_ref, f32[16,3,256,128]{3,2,1,0:T(8,128)} %all-gather.13.cloned.1.call-done.gain_ref, f32[4,256,4096]{2,1,0:T(8,128)} %noise_ref.7, ...), custom_call_target="tpu_custom_call", output_to_operand_aliasing={{0}: (6, {})} | custom-call | tf_op jit(solution)/shard_map/left_product/pallas_call | solution.py:132
  665.0 0.0 copy-done
  665.0 0.0 copy-done.1
  665.0 0.0 copy-done.2
  665.0 1.3 fusion.2
  (1 shorter events, 0.0 us)
Async XLA Ops:
  7.2 66.2 %all-gather.7.cloned.1.call-start = ((), (), s32[]{:S(2)}) async-start(), calls=%async_computation.4 | async-start | bytes 6684672 | tf_op jit(solution)/shard_map/all_gather | solution.py:158
  9.7 239.8 %all-gather.9.cloned.1.call-start = ((), (), s32[]{:S(2)}) async-start(), calls=%async_computation.5 | async-start | bytes 6684672 | tf_op jit(solution)/shard_map/all_gather | solution.py:158
  86.3 6.5 copy-start.3
  86.3 6.5 copy-start.4
  86.3 148.4 %all-to-all-start = ((f32[16,256,256]{2,1,0:T(8,128)}), f32[16,256,256]{2,1,0:T(8,128)}, u32[]{:S(2)}, u32[]{:S(2)}) async-start(f32[16,256,256]{2,1,0:T(8,128)} %right_product.4), calls=%async_computation | async-start | bytes 8388608 | tf_op jit(solution)/shard_map/all_to_all | solution.py:169
  92.1 322.6 %all-gather.11.cloned.1.call-start = ((), (), s32[]{:S(2)}) async-start(), calls=%async_computation.6 | async-start | bytes 6684672 | tf_op jit(solution)/shard_map/all_gather | solution.py:158
  262.8 137.2 %all-to-all-start.1 = ((f32[16,256,256]{2,1,0:T(8,128)}), f32[16,256,256]{2,1,0:T(8,128)}, u32[]{:S(2)}, u32[]{:S(2)}) async-start(f32[16,256,256]{2,1,0:T(8,128)} %right_product.5), calls=%async_computation.1 | async-start | bytes 8388608 | tf_op jit(solution)/shard_map/all_to_all | solution.py:169
  269.3 270.0 %all-gather.13.cloned.1.call-start = ((), (), s32[]{:S(2)}) async-start(), calls=%async_computation.7 | async-start | bytes 6684672 | tf_op jit(solution)/shard_map/all_gather | solution.py:158
  552.3 97.8 %all-to-all-start.3 = ((f32[16,256,256]{2,1,0:T(8,128)}), f32[16,256,256]{2,1,0:T(8,128)}, u32[]{:S(2)}, u32[]{:S(2)}) async-start(f32[16,256,256]{2,1,0:T(8,128)} %right_product.7), calls=%async_computation.3 | async-start | bytes 8388608 | tf_op jit(solution)/shard_map/all_to_all | solution.py:169
  650.1 14.9 %copy-start = (f32[32,1,128]{2,1,0:T(1,128)S(1)}, f32[32,1,128]{2,1,0:T(1,128)}, u32[]{:S(2)}) copy-start(f32[32,1,128]{2,1,0:T(1,128)} %get-tuple-element.11.mean_ref) | copy-start | bytes 49156
  650.1 14.9 %copy-start.1 = (f32[32,1,128]{2,1,0:T(1,128)S(1)}, f32[32,1,128]{2,1,0:T(1,128)}, u32[]{:S(2)}) copy-start(f32[32,1,128]{2,1,0:T(1,128)} %get-tuple-element.13.mean_ref) | copy-start | bytes 49156
  650.1 14.9 %copy-start.2 = (f32[32,1,128]{2,1,0:T(1,128)S(1)}, f32[32,1,128]{2,1,0:T(1,128)}, u32[]{:S(2)}) copy-start(f32[32,1,128]{2,1,0:T(1,128)} %get-tuple-element.15.mean_ref) | copy-start | bytes 49156
Sparse Core Ops, SparseCore 0:
  10.9 62.4 all-gather.6
  75.6 115.3 all-gather.8
  193.3 70.5 all-gather.10
  272.1 110.6 all-gather.12

commit v2 on v1

--- a/solution.py
+++ b/solution.py
@@ -33,8 +33,20 @@
 
 
 def gain_parts(gain_ref):
-    parts = [gain_ref[:, k].reshape(STEP, TILE) for k in range(PER_ROW)]
-    return split(jnp.concatenate(parts, axis=1))
+    cores, chips = gain_ref.shape[:2]
+    rows = [
+        jnp.concatenate([gain_ref[c, i, k] for k in range(PER_ROW)], axis=1)
+        for i in range(chips)
+        for c in range(cores)
+    ]
+    return split(jnp.concatenate(rows, axis=0))
+
+
+def gather_gain(gain, n):
+    same_core = [[2 * i + c for i in range(n // 2)] for c in range(2)]
+    same_chip = [[2 * i, 2 * i + 1] for i in range(n // 2)]
+    half = lax.all_gather(gain, "rows", axis_index_groups=same_core)
+    return lax.all_gather(half, "rows", axis_index_groups=same_chip)
 
 
 def picked(ref, pattern_ref, block, tile):
@@ -103,7 +115,7 @@
             grid=(STEPS,),
             in_specs=[
                 cov_spec,
-                pl.BlockSpec((per, PER_ROW, local, TILE), lambda i, s: (i, 0, 0, 0)),
+                pl.BlockSpec((2, per // 2, PER_ROW, local, TILE), lambda i, s: (0, i, 0, 0, 0)),
             ],
             out_specs=pl.BlockSpec((per, local, local), lambda i, s: (i, 0, 0)),
             scratch_shapes=[pltpu.VMEM((TILE_ROWS, local, TILE), jnp.bfloat16)] * 2,
@@ -118,7 +130,7 @@
     tiles = STEP // TILE
     in_specs = [
         pl.BlockSpec((n, local, local), lambda i, s: (0, 0, 0)),
-        pl.BlockSpec((per, PER_ROW, local, TILE), lambda i, s: (i, 0, 0, 0)),
+        pl.BlockSpec((2, per // 2, PER_ROW, local, TILE), lambda i, s: (0, i, 0, 0, 0)),
         pl.BlockSpec((None, local, STEP), lambda i, s: (block, 0, i)),
         pl.BlockSpec((TILE_ROWS, 1, TILE), lambda i, s: (0, 0, 0)),
         pl.BlockSpec((tiles, 1, TILE), lambda i, s: (i, 0, 0)),
@@ -155,7 +167,7 @@
     local = last_mean.shape[0]
     pattern = tile_pattern.reshape(-1)
     gains = jnp.transpose(gain_tiles, (0, 2, 1, 3))
-    gathered = {b: lax.all_gather(gains[b], "rows") for b in reversed(range(BLOCKS))}
+    gathered = {b: gather_gain(gains[b], n) for b in reversed(range(BLOCKS))}
     vectors = lax.all_gather(jnp.concatenate([offset_terms, last_mean[None]], 0), "rows")
     vectors = jnp.transpose(vectors, (1, 0, 2)).reshape(BLOCKS + 1, TILE_ROWS, 1, TILE)
     mean = vectors[BLOCKS]

time: 675 us -> 743 us (1.10)
  waiting for transfers between devices: 286 us -> 554 us
  blocking collectives: 238 us -> 34 us
    all_gather x4 -> x8, waiting for transfers between devices: 61.3 us -> 237 us  [the longest x4 218 us: gather_gain(): half = lax.all_gather(gain, 'rows', axis_index_groups=same_core)]
    all_gather x1, blocking collectives: 141 us -> 34 us  [shards(): lax.all_gather(jnp.concatenate([offset_terms, last_mean[None]], 0), 'rows')]
    all_to_all x1 -> x0, blocking collectives: 96.9 us -> none  [shards(): recv = lax.all_to_all(send, 'rows', split_axis=0, concat_axis=0, tiled=True)]
    all_to_all x3 -> x4, waiting for transfers between devices: 223 us -> 314 us  [shards(): recv = lax.all_to_all(send, 'rows', split_axis=0, concat_axis=0, tiled=True)]
    all_to_all x3 -> x4, starting transfers between devices: 17.6 us -> 21.5 us  [shards(): recv = lax.all_to_all(send, 'rows', split_axis=0, concat_axis=0, tiled=True)]
  transfers between devices with their start and end apart: 7 -> 12, of which waited for: 3 -> 7; matrix products, arithmetic and copies ran while one was open for 0% -> 0% of each run, Pallas kernels for 12% -> 11%
where the time goes in v2:
time: 743 us; the launch traced here: 740 us
  waiting for transfers between devices  554 us (75%)
  Pallas kernels  111 us (15%)
  blocking collectives  34 us (5%)
  starting transfers between devices  21.8 us (3%)
  between operations  14.2 us (2%)
    all_to_all x4, waiting for transfers between devices, shards(): recv = lax.all_to_all(send, 'rows', split_axis=0, concat_axis=0, tiled=True)  314 us
    all_gather x4, waiting for transfers between devices, gather_gain(): half = lax.all_gather(gain, 'rows', axis_index_groups=same_core)  218 us
    pallas_call x4, Pallas kernels, left(): pl.pallas_call(functools.partial(left_kernel, block), out_shape=(jax.Shap...  58.8 us
    pallas_call x4, Pallas kernels, right(): pl.pallas_call(functools.partial(right_kernel, block), out_shape=jax.Shap...  52 us
    all_gather x1, blocking collectives, shards(): lax.all_gather(jnp.concatenate([offset_terms, last_mean[None]], 0), 'rows')  34 us
    all_to_all x4, starting transfers between devices, shards(): recv = lax.all_to_all(send, 'rows', split_axis=0, concat_axis=0, tiled=True)  21.5 us
    all_gather x4, waiting for transfers between devices, gather_gain(): return lax.all_gather(half, 'rows', axis_index_groups=same_chip)  19 us
  transfers between devices with their start and end apart: 12, of which 7 were waited for; matrix products, arithmetic and copies ran while one was open for 0% of the time, Pallas kernels for 11%

profile of v2, /device:TPU:13, one launch (start us, length us, event | category | flops | bytes accessed | tf_op | source)
XLA Modules:
  0.0 740.4 jit_solution(10742699259363887334)
XLA Ops:
  7.2 0.0 all-gather.15.cloned.1.call-start
  7.2 2.5 fusion.3
  9.7 0.0 all-gather.15.cloned.1.call-update
  9.7 0.0 all-gather.17.cloned.1.call-start
  9.8 0.7 all-gather.17.cloned.1.call-update
  10.5 0.0 all-gather.23.cloned.1.call-start
  10.5 59.0 %all-gather.15.cloned.1.call-done = f32[8,3,256,128]{3,2,1,0:T(8,128)} async-done(((f32[1,3,256,128]{3,2,1,0:T(8,128)}), f32[8,3,256,128]{3,2,1,0:T(8,128)}) %all-gather.15.cloned.1.call-update) | async-done | bytes 3145744 | tf_op jit(solution)/shard_map/all_gather | solution.py:48
  69.6 0.0 all-gather.23.cloned.1.call-update
  69.6 0.0 all-gather.19.cloned.1.call-start
  69.7 0.5 all-gather.19.cloned.1.call-update
  70.2 0.0 all-gather.25.cloned.1.call-start
  70.2 61.2 %all-gather.17.cloned.1.call-done = f32[8,3,256,128]{3,2,1,0:T(8,128)} async-done(((f32[1,3,256,128]{3,2,1,0:T(8,128)}), f32[8,3,256,128]{3,2,1,0:T(8,128)}) %all-gather.17.cloned.1.call-update) | async-done | bytes 3145744 | tf_op jit(solution)/shard_map/all_gather | solution.py:48
  131.5 0.0 all-gather.25.cloned.1.call-update
  131.5 0.0 copy-done.3
  131.5 0.1 copy.12
  131.6 0.8 reshape.18.pattern_ref
  132.4 18.9 %all-gather.23.cloned.1.call-done = f32[16,3,256,128]{3,2,1,0:T(8,128)} async-done(((f32[8,3,256,128]{3,2,1,0:T(8,128)}), f32[16,3,256,128]{3,2,1,0:T(8,128)}) %all-gather.23.cloned.1.call-update) | async-done | bytes 6291472 | tf_op jit(solution)/shard_map/all_gather | solution.py:49
  151.3 13.0 %right_product.4 = f32[16,256,256]{2,1,0:T(8,128)} custom-call(s32[384]{0:T(512)} %reshape.18.pattern_ref, f32[256,4096]{1,0:T(8,128)} %cov_ref.1, f32[2,8,3,256,128]{4,3,2,1,0:T(8,128)} %bitcast.24), custom_call_target="tpu_custom_call" | custom-call | tf_op jit(solution)/shard_map/right_product/pallas_call | solution.py:110
  164.4 6.0 all-to-all-start
  170.4 0.0 all-gather.27.cloned.1.call-start
  170.4 98.1 %all-gather.19.cloned.1.call-done = f32[8,3,256,128]{3,2,1,0:T(8,128)} async-done(((f32[1,3,256,128]{3,2,1,0:T(8,128)}), f32[8,3,256,128]{3,2,1,0:T(8,128)}) %all-gather.19.cloned.1.call-update) | async-done | bytes 3145744 | tf_op jit(solution)/shard_map/all_gather | solution.py:48
  268.5 0.0 all-gather.27.cloned.1.call-update
  268.6 0.0 copy-done.4
  268.6 0.0 copy-done.5
  268.6 34.0 %all-gather.5 = f32[16,5,256]{2,1,0:T(8,128)S(1)} all-gather(f32[1,5,256]{2,1,0:T(8,128)S(1)} %maximum_bitcast_fusion), channel_id=3, replica_groups=mesh['parts'=2,'rows'=16] {'rows'}, dimensions={0}, use_global_device_ids=true | all-gather | bytes 87040 | tf_op jit(solution)/shard_map/all_gather | solution.py:171
  302.6 0.7 fusion.4
  303.3 0.0 all-to-all-done.recv_ref
  303.3 15.1 %left_product.4 = (f32[4,256,4096]{2,1,0:T(8,128)}, f32[32,1,128]{2,1,0:T(1,128)}) custom-call(s32[384]{0:T(512)} %reshape.18.pattern_ref, f32[16,256,256]{2,1,0:T(8,128)} %all-to-all-done.recv_ref, f32[2,8,3,256,128]{4,3,2,1,0:T(8,128)} %bitcast.25, f32[4,256,4096]{2,1,0:T(8,128)} %noise_ref.7, f32[32,1,128]{2,1,0:T(1,128)} %bitcast.35, f32[32,1,128]{2,1,0:T(1,128)} %bitcast.34), custom_call_target="tpu_custom_call" | custom-call | tf_op jit(solution)/shard_map/left_product/pallas_call | solution.py:144
  318.4 13.0 %right_product.5 = f32[16,256,256]{2,1,0:T(8,128)} custom-call(s32[384]{0:T(512)} %reshape.18.pattern_ref, f32[4,256,4096]{2,1,0:T(8,128)} %get-tuple-element.10.cov_ref.rest_0_, f32[2,8,3,256,128]{4,3,2,1,0:T(8,128)} %bitcast.20), custom_call_target="tpu_custom_call" | custom-call | tf_op jit(solution)/shard_map/right_product/pallas_call | solution.py:110
  331.4 5.5 all-to-all-start.1
  336.9 0.0 all-gather.21.cloned.1.call-start
  337.0 0.7 all-gather.21.cloned.1.call-update
  337.7 129.9 %all-to-all-done.1.recv_ref = f32[16,256,256]{2,1,0:T(8,128)} async-done(((f32[16,256,256]{2,1,0:T(8,128)}), f32[16,256,256]{2,1,0:T(8,128)}, u32[]{:S(2)}, u32[]{:S(2)}) %all-to-all-start.1) | async-done | bytes 4194336 | tf_op jit(solution)/shard_map/all_to_all | solution.py:181
  467.6 14.5 %left_product.5 = (f32[4,256,4096]{2,1,0:T(8,128)}, f32[32,1,128]{2,1,0:T(1,128)}) custom-call(s32[384]{0:T(512)} %reshape.18.pattern_ref, f32[16,256,256]{2,1,0:T(8,128)} %all-to-all-done.1.recv_ref, f32[2,8,3,256,128]{4,3,2,1,0:T(8,128)} %bitcast.21, f32[4,256,4096]{2,1,0:T(8,128)} %noise_ref.7, ...), custom_call_target="tpu_custom_call", output_to_operand_aliasing={{0}: (6, {})} | custom-call | tf_op jit(solution)/shard_map/left_product/pallas_call | solution.py:144
  482.1 13.0 %right_product.6 = f32[16,256,256]{2,1,0:T(8,128)} custom-call(s32[384]{0:T(512)} %reshape.18.pattern_ref, f32[4,256,4096]{2,1,0:T(8,128)} %get-tuple-element.12.cov_ref.rest_0_, f32[2,8,3,256,128]{4,3,2,1,0:T(8,128)} %bitcast.18), custom_call_target="tpu_custom_call" | custom-call | tf_op jit(solution)/shard_map/right_product/pallas_call | solution.py:110
  495.1 5.1 all-to-all-start.2
  500.2 0.0 all-gather.29.cloned.1.call-start
  500.2 0.0 all-gather.21.cloned.1.call-done
  500.3 0.7 all-gather.29.cloned.1.call-update
  500.9 91.7 %all-to-all-done.2.recv_ref = f32[16,256,256]{2,1,0:T(8,128)} async-done(((f32[16,256,256]{2,1,0:T(8,128)}), f32[16,256,256]{2,1,0:T(8,128)}, u32[]{:S(2)}, u32[]{:S(2)}) %all-to-all-start.2) | async-done | bytes 4194336 | tf_op jit(solution)/shard_map/all_to_all | solution.py:181
  592.6 14.5 %left_product.6 = (f32[4,256,4096]{2,1,0:T(8,128)}, f32[32,1,128]{2,1,0:T(1,128)}) custom-call(s32[384]{0:T(512)} %reshape.18.pattern_ref, f32[16,256,256]{2,1,0:T(8,128)} %all-to-all-done.2.recv_ref, f32[2,8,3,256,128]{4,3,2,1,0:T(8,128)} %bitcast.19, f32[4,256,4096]{2,1,0:T(8,128)} %noise_ref.7, ...), custom_call_target="tpu_custom_call", output_to_operand_aliasing={{0}: (6, {})} | custom-call | tf_op jit(solution)/shard_map/left_product/pallas_call | solution.py:144
  607.2 13.0 %right_product.7 = f32[16,256,256]{2,1,0:T(8,128)} custom-call(s32[384]{0:T(512)} %reshape.18.pattern_ref, f32[4,256,4096]{2,1,0:T(8,128)} %get-tuple-element.14.cov_ref.rest_0_, f32[2,8,3,256,128]{4,3,2,1,0:T(8,128)} %bitcast.22), custom_call_target="tpu_custom_call" | custom-call | tf_op jit(solution)/shard_map/right_product/pallas_call | solution.py:110
  620.2 4.9 all-to-all-start.3
  625.1 92.5 %all-to-all-done.3.recv_ref = f32[16,256,256]{2,1,0:T(8,128)} async-done(((f32[16,256,256]{2,1,0:T(8,128)}), f32[16,256,256]{2,1,0:T(8,128)}, u32[]{:S(2)}, u32[]{:S(2)}) %all-to-all-start.3) | async-done | bytes 4194336 | tf_op jit(solution)/shard_map/all_to_all | solution.py:181
  717.6 14.7 %left_product.7 = (f32[4,256,4096]{2,1,0:T(8,128)}, f32[32,1,128]{2,1,0:T(1,128)}) custom-call(s32[384]{0:T(512)} %reshape.18.pattern_ref, f32[16,256,256]{2,1,0:T(8,128)} %all-to-all-done.3.recv_ref, f32[2,8,3,256,128]{4,3,2,1,0:T(8,128)} %bitcast.23, f32[4,256,4096]{2,1,0:T(8,128)} %noise_ref.7, ...), custom_call_target="tpu_custom_call", output_to_operand_aliasing={{0}: (6, {})} | custom-call | tf_op jit(solution)/shard_map/left_product/pallas_call | solution.py:144
  732.2 0.0 copy-done
  732.2 0.0 copy-done.1
  732.3 1.3 fusion.2
  (11 shorter events, 0.0 us)
Async XLA Ops:
  7.2 62.4 %all-gather.15.cloned.1.call-start = ((), (), s32[]{:S(2)}) async-start(), calls=%async_computation.4 | async-start | bytes 3538944 | tf_op jit(solution)/shard_map/all_gather | solution.py:48
  9.7 121.8 %copy-start.3 = (s32[4,32,3]{1,0,2:T(4,128)S(1)}, s32[4,32,3]{1,0,2:T(4,128)}, u32[]{:S(2)}) copy-start(s32[4,32,3]{1,0,2:T(4,128)} %param.7) | copy-start | bytes 4612
  9.7 121.7 %all-gather.17.cloned.1.call-start = ((), (), s32[]{:S(2)}) async-start(), calls=%async_computation.5 | async-start | bytes 3538944 | tf_op jit(solution)/shard_map/all_gather | solution.py:48
  10.5 140.8 %all-gather.23.cloned.1.call-start = ((), (), s32[]{:S(2)}) async-start(), calls=%async_computation.8 | async-start | bytes 9437184 | tf_op jit(solution)/shard_map/all_gather | solution.py:49
  69.6 198.9 %all-gather.19.cloned.1.call-start = ((), (), s32[]{:S(2)}) async-start(), calls=%async_computation.6 | async-start | bytes 3538944 | tf_op jit(solution)/shard_map/all_gather | solution.py:48
  70.2 248.2 %all-gather.25.cloned.1.call-start = ((), (), s32[]{:S(2)}) async-start(), calls=%async_computation.9 | async-start | bytes 9437184 | tf_op jit(solution)/shard_map/all_gather | solution.py:49
  164.4 104.2 %copy-start.4 = (f32[4,256]{1,0:T(4,128)S(1)}, f32[4,256]{1,0:T(4,128)}, u32[]{:S(2)}) copy-start(f32[4,256]{1,0:T(4,128)} %param.8) | copy-start | bytes 12292
  164.4 104.2 %copy-start.5 = (f32[256]{0:T(256)S(1)}, f32[256]{0:T(256)}, u32[]{:S(2)}) copy-start(f32[256]{0:T(256)} %param.9) | copy-start | bytes 3076
  164.4 138.9 %all-to-all-start = ((f32[16,256,256]{2,1,0:T(8,128)}), f32[16,256,256]{2,1,0:T(8,128)}, u32[]{:S(2)}, u32[]{:S(2)}) async-start(f32[16,256,256]{2,1,0:T(8,128)} %right_product.4), calls=%async_computation | async-start | bytes 8388608 | tf_op jit(solution)/shard_map/all_to_all | solution.py:181
  170.4 311.7 %all-gather.27.cloned.1.call-start = ((), (), s32[]{:S(2)}) async-start(), calls=%async_computation.10 | async-start | bytes 9437184 | tf_op jit(solution)/shard_map/all_gather | solution.py:49
  331.4 136.2 %all-to-all-start.1 = ((f32[16,256,256]{2,1,0:T(8,128)}), f32[16,256,256]{2,1,0:T(8,128)}, u32[]{:S(2)}, u32[]{:S(2)}) async-start(f32[16,256,256]{2,1,0:T(8,128)} %right_product.5), calls=%async_computation.1 | async-start | bytes 8388608 | tf_op jit(solution)/shard_map/all_to_all | solution.py:181
  336.9 163.3 %all-gather.21.cloned.1.call-start = ((), (), s32[]{:S(2)}) async-start(), calls=%async_computation.7 | async-start | bytes 3538944 | tf_op jit(solution)/shard_map/all_gather | solution.py:48
  495.1 97.6 %all-to-all-start.2 = ((f32[16,256,256]{2,1,0:T(8,128)}), f32[16,256,256]{2,1,0:T(8,128)}, u32[]{:S(2)}, u32[]{:S(2)}) async-start(f32[16,256,256]{2,1,0:T(8,128)} %right_product.6), calls=%async_computation.2 | async-start | bytes 8388608 | tf_op jit(solution)/shard_map/all_to_all | solution.py:181
  500.2 107.0 %all-gather.29.cloned.1.call-start = ((), (), s32[]{:S(2)}) async-start(), calls=%async_computation.11 | async-start | bytes 9437184 | tf_op jit(solution)/shard_map/all_gather | solution.py:49
  620.2 97.4 %all-to-all-start.3 = ((f32[16,256,256]{2,1,0:T(8,128)}), f32[16,256,256]{2,1,0:T(8,128)}, u32[]{:S(2)}, u32[]{:S(2)}) async-start(f32[16,256,256]{2,1,0:T(8,128)} %right_product.7), calls=%async_computation.3 | async-start | bytes 8388608 | tf_op jit(solution)/shard_map/all_to_all | solution.py:181
  717.6 14.7 %copy-start = (f32[32,1,128]{2,1,0:T(1,128)S(1)}, f32[32,1,128]{2,1,0:T(1,128)}, u32[]{:S(2)}) copy-start(f32[32,1,128]{2,1,0:T(1,128)} %get-tuple-element.11.mean_ref) | copy-start | bytes 49156
  717.6 14.7 %copy-start.1 = (f32[32,1,128]{2,1,0:T(1,128)S(1)}, f32[32,1,128]{2,1,0:T(1,128)}, u32[]{:S(2)}) copy-start(f32[32,1,128]{2,1,0:T(1,128)} %get-tuple-element.13.mean_ref) | copy-start | bytes 49156
  717.6 14.7 %copy-start.2 = (f32[32,1,128]{2,1,0:T(1,128)S(1)}, f32[32,1,128]{2,1,0:T(1,128)}, u32[]{:S(2)}) copy-start(f32[32,1,128]{2,1,0:T(1,128)} %get-tuple-element.15.mean_ref) | copy-start | bytes 49156
Sparse Core Ops, SparseCore 0:
  10.2 59.3 all-gather.14
  72.3 59.0 all-gather.16
  133.0 18.2 all-gather.22
  153.4 115.1 all-gather.18
  269.9 21.9 all-gather.24
  293.3 17.9 all-gather.26
  339.9 110.3 all-gather.20
  502.6 18.0 all-gather.28

commit v3 on v1

--- a/solution.py
+++ b/solution.py
@@ -155,7 +155,7 @@
     local = last_mean.shape[0]
     pattern = tile_pattern.reshape(-1)
     gains = jnp.transpose(gain_tiles, (0, 2, 1, 3))
-    gathered = {b: lax.all_gather(gains[b], "rows") for b in reversed(range(BLOCKS))}
+    gathered = {BLOCKS - 1: lax.all_gather(gains[BLOCKS - 1], "rows")}
     vectors = lax.all_gather(jnp.concatenate([offset_terms, last_mean[None]], 0), "rows")
     vectors = jnp.transpose(vectors, (1, 0, 2)).reshape(BLOCKS + 1, TILE_ROWS, 1, TILE)
     mean = vectors[BLOCKS]
@@ -166,6 +166,9 @@
             send = right(b, pattern, last_covariance, None, gathered[b], n, local)
         else:
             send = right(b, pattern, stack, b + 1, gathered[b], n, local)
+        if b > 0:
+            send, gain = lax.optimization_barrier((send, gains[b - 1]))
+            gathered[b - 1] = lax.all_gather(gain, "rows")
         recv = lax.all_to_all(send, "rows", split_axis=0, concat_axis=0, tiled=True)
         stack, mean = left(
             b, pattern, recv, gathered[b], noise_covariance, mean, vectors[b], stack, n, local

time: 675 us -> 709 us (1.050)
  blocking collectives: 238 us -> 411 us
  waiting for transfers between devices: 286 us -> 154 us
    all_to_all x1 -> x2, blocking collectives: 96.9 us -> 271 us  [shards(): recv = lax.all_to_all(send, 'rows', split_axis=0, concat_axis=0, tiled=True)]
    all_to_all x3 -> x2, waiting for transfers between devices: 223 us -> 92.5 us  [shards(): recv = lax.all_to_all(send, 'rows', split_axis=0, concat_axis=0, tiled=True)]
    all_to_all x3 -> x2, starting transfers between devices: 17.6 us -> 10.7 us  [shards(): recv = lax.all_to_all(send, 'rows', split_axis=0, concat_axis=0, tiled=True)]
  transfers between devices with their start and end apart: 7 -> 6, of which waited for: 3 -> 2; matrix products, arithmetic and copies ran while one was open for 0% -> 0% of each run, Pallas kernels for 12% -> 6%
where the time goes in v3:
time: 709 us; the launch traced here: 707 us
  blocking collectives  411 us (58%)
  waiting for transfers between devices  154 us (22%)
  Pallas kernels  111 us (16%)
  between operations  13.8 us (2%)
  starting transfers between devices  10.9 us (2%)
    all_to_all x2, blocking collectives, shards(): recv = lax.all_to_all(send, 'rows', split_axis=0, concat_axis=0, tiled=True)  271 us
    all_gather x1, blocking collectives, shards(): lax.all_gather(jnp.concatenate([offset_terms, last_mean[None]], 0), 'rows')  140 us
    all_to_all x2, waiting for transfers between devices, shards(): recv = lax.all_to_all(send, 'rows', split_axis=0, concat_axis=0, tiled=True)  92.5 us
    all_gather x1, waiting for transfers between devices, shards(): gathered = {BLOCKS - 1: lax.all_gather(gains[BLOCKS - 1], 'rows')}  62 us
    pallas_call x4, Pallas kernels, left(): pl.pallas_call(functools.partial(left_kernel, block), out_shape=(jax.Shap...  59 us
    pallas_call x4, Pallas kernels, right(): pl.pallas_call(functools.partial(right_kernel, block), out_shape=jax.Shap...  51.8 us
  transfers between devices with their start and end apart: 6, of which 2 were waited for; matrix products, arithmetic and copies ran while one was open for 0% of the time, Pallas kernels for 6%

profile of v3, /device:TPU:13, one launch (start us, length us, event | category | flops | bytes accessed | tf_op | source)
XLA Modules:
  0.0 707.2 jit_solution(2614840472899866993)
XLA Ops:
  7.2 0.0 all-gather.10.cloned.1.call-start
  7.2 2.5 slice_bitcast_fusion
  9.7 0.0 all-gather.10.cloned.1.call-update
  9.7 0.0 all-gather.12.cloned.1.call-start
  9.8 0.8 copy.12
  10.6 0.8 reshape.18.pattern_ref
  11.4 62.0 %all-gather.10.cloned.1.call-done.gain_ref = f32[16,3,256,128]{3,2,1,0:T(8,128)} async-done(((f32[1,3,256,128]{3,2,1,0:T(8,128)}), f32[16,3,256,128]{3,2,1,0:T(8,128)}) %all-gather.10.cloned.1.call-update) | async-done | bytes 6291472 | tf_op jit(solution)/shard_map/all_gather | solution.py:158
  73.3 12.9 %right_product.4 = f32[16,256,256]{2,1,0:T(8,128)} custom-call(s32[384]{0:T(512)} %reshape.18.pattern_ref, f32[256,4096]{1,0:T(8,128)} %cov_ref.1, f32[16,3,256,128]{3,2,1,0:T(8,128)} %all-gather.10.cloned.1.call-done.gain_ref), custom_call_target="tpu_custom_call" | custom-call | tf_op jit(solution)/shard_map/right_product/pallas_call | solution.py:98
  86.3 0.0 all-gather.12.cloned.1.call-update
  86.3 0.0 copy-start.3
  86.3 0.0 copy-start.4
  86.3 5.7 all-to-all-start
  92.0 0.0 all-gather.14.cloned.1.call-start
  92.0 0.0 copy-done.3
  92.1 0.0 copy-done.4
  92.1 140.0 %all-gather.4 = f32[16,5,256]{2,1,0:T(8,128)S(1)} all-gather(f32[1,5,256]{2,1,0:T(8,128)S(1)} %maximum_bitcast_fusion), channel_id=2, replica_groups=mesh['parts'=2,'rows'=16] {'rows'}, dimensions={0}, use_global_device_ids=true | all-gather | bytes 87040 | tf_op jit(solution)/shard_map/all_gather | solution.py:159
  232.1 0.7 fusion.3
  232.7 0.0 all-to-all-done.recv_ref
  232.7 14.7 %left_product.4 = (f32[4,256,4096]{2,1,0:T(8,128)}, f32[32,1,128]{2,1,0:T(1,128)}) custom-call(s32[384]{0:T(512)} %reshape.18.pattern_ref, f32[16,256,256]{2,1,0:T(8,128)} %all-to-all-done.recv_ref, f32[16,3,256,128]{3,2,1,0:T(8,128)} %all-gather.10.cloned.1.call-done.gain_ref, f32[4,256,4096]{2,1,0:T(8,128)} %noise_ref.7, f32[32,1,128]{2,1,0:T(1,128)} %bitcast.38, ...), custom_call_target="tpu_custom_call" | custom-call | tf_op jit(solution)/shard_map/left_product/pallas_call | solution.py:132
  247.4 0.0 all-gather.12.cloned.1.call-done
  247.4 12.9 %right_product.5 = f32[16,256,256]{2,1,0:T(8,128)} custom-call(s32[384]{0:T(512)} %reshape.18.pattern_ref, f32[4,256,4096]{2,1,0:T(8,128)} %get-tuple-element.17.cov_ref.rest_0_, f32[16,3,256,128]{3,2,1,0:T(8,128)} %bitcast.23), custom_call_target="tpu_custom_call" | custom-call | tf_op jit(solution)/shard_map/right_product/pallas_call | solution.py:98
  260.4 0.0 all-gather.14.cloned.1.call-update
  260.4 0.0 all-gather.16.cloned.1.call-start
  260.4 135.7 %all_to_all.20.recv_ref = f32[16,256,256]{2,1,0:T(8,128)} all-to-all(f32[16,256,256]{2,1,0:T(8,128)} %right_product.5), channel_id=1, replica_groups=mesh['parts'=2,'rows'=16] {'rows'}, dimensions={0} | all-to-all | bytes 8388608 | tf_op jit(solution)/shard_map/all_to_all | solution.py:172
  396.2 14.7 %left_product.5 = (f32[4,256,4096]{2,1,0:T(8,128)}, f32[32,1,128]{2,1,0:T(1,128)}) custom-call(s32[384]{0:T(512)} %reshape.18.pattern_ref, f32[16,256,256]{2,1,0:T(8,128)} %all_to_all.20.recv_ref, f32[16,3,256,128]{3,2,1,0:T(8,128)} %bitcast.24, f32[4,256,4096]{2,1,0:T(8,128)} %noise_ref.7, ...), custom_call_target="tpu_custom_call", output_to_operand_aliasing={{0}: (6, {})} | custom-call | tf_op jit(solution)/shard_map/left_product/pallas_call | solution.py:132
  410.9 0.0 all-gather.14.cloned.1.call-done
  410.9 12.9 %right_product.6 = f32[16,256,256]{2,1,0:T(8,128)} custom-call(s32[384]{0:T(512)} %reshape.18.pattern_ref, f32[4,256,4096]{2,1,0:T(8,128)} %get-tuple-element.21.cov_ref.rest_0_, f32[16,3,256,128]{3,2,1,0:T(8,128)} %bitcast.27), custom_call_target="tpu_custom_call" | custom-call | tf_op jit(solution)/shard_map/right_product/pallas_call | solution.py:98
  423.8 0.0 all-gather.16.cloned.1.call-update
  423.8 135.4 %all_to_all.21.recv_ref = f32[16,256,256]{2,1,0:T(8,128)} all-to-all(f32[16,256,256]{2,1,0:T(8,128)} %right_product.6), channel_id=1, replica_groups=mesh['parts'=2,'rows'=16] {'rows'}, dimensions={0} | all-to-all | bytes 8388608 | tf_op jit(solution)/shard_map/all_to_all | solution.py:172
  559.2 14.7 %left_product.6 = (f32[4,256,4096]{2,1,0:T(8,128)}, f32[32,1,128]{2,1,0:T(1,128)}) custom-call(s32[384]{0:T(512)} %reshape.18.pattern_ref, f32[16,256,256]{2,1,0:T(8,128)} %all_to_all.21.recv_ref, f32[16,3,256,128]{3,2,1,0:T(8,128)} %bitcast.28, f32[4,256,4096]{2,1,0:T(8,128)} %noise_ref.7, ...), custom_call_target="tpu_custom_call", output_to_operand_aliasing={{0}: (6, {})} | custom-call | tf_op jit(solution)/shard_map/left_product/pallas_call | solution.py:132
  573.9 0.0 all-gather.16.cloned.1.call-done
  573.9 13.0 %right_product.7 = f32[16,256,256]{2,1,0:T(8,128)} custom-call(s32[384]{0:T(512)} %reshape.18.pattern_ref, f32[4,256,4096]{2,1,0:T(8,128)} %get-tuple-element.25.cov_ref.rest_0_, f32[16,3,256,128]{3,2,1,0:T(8,128)} %bitcast.25), custom_call_target="tpu_custom_call" | custom-call | tf_op jit(solution)/shard_map/right_product/pallas_call | solution.py:98
  587.0 5.0 all-to-all-start.3
  592.0 92.5 %all-to-all-done.3.recv_ref = f32[16,256,256]{2,1,0:T(8,128)} async-done(((f32[16,256,256]{2,1,0:T(8,128)}), f32[16,256,256]{2,1,0:T(8,128)}, u32[]{:S(2)}, u32[]{:S(2)}) %all-to-all-start.3) | async-done | bytes 4194336 | tf_op jit(solution)/shard_map/all_to_all | solution.py:172
  684.5 0.0 copy-start
  684.5 0.0 copy-start.1
  684.5 0.0 copy-start.2
  684.5 14.9 %left_product.7 = (f32[4,256,4096]{2,1,0:T(8,128)}, f32[32,1,128]{2,1,0:T(1,128)}) custom-call(s32[384]{0:T(512)} %reshape.18.pattern_ref, f32[16,256,256]{2,1,0:T(8,128)} %all-to-all-done.3.recv_ref, f32[16,3,256,128]{3,2,1,0:T(8,128)} %bitcast.26, f32[4,256,4096]{2,1,0:T(8,128)} %noise_ref.7, ...), custom_call_target="tpu_custom_call", output_to_operand_aliasing={{0}: (6, {})} | custom-call | tf_op jit(solution)/shard_map/left_product/pallas_call | solution.py:132
  699.3 0.0 copy-done
  699.3 0.0 copy-done.1
  699.4 0.0 copy-done.2
  699.4 1.3 fusion.2
  (1 shorter events, 0.0 us)
Async XLA Ops:
  7.2 66.2 %all-gather.10.cloned.1.call-start = ((), (), s32[]{:S(2)}) async-start(), calls=%async_computation.4 | async-start | bytes 6684672 | tf_op jit(solution)/shard_map/all_gather | solution.py:158
  9.7 237.7 %all-gather.12.cloned.1.call-start = ((), (), s32[]{:S(2)}) async-start(), calls=%async_computation.5 | async-start | bytes 6684672 | tf_op jit(solution)/shard_map/all_gather | solution.py:171
  86.3 5.7 copy-start.3
  86.3 5.7 copy-start.4
  86.3 146.4 %all-to-all-start = ((f32[16,256,256]{2,1,0:T(8,128)}), f32[16,256,256]{2,1,0:T(8,128)}, u32[]{:S(2)}, u32[]{:S(2)}) async-start(f32[16,256,256]{2,1,0:T(8,128)} %right_product.4), calls=%async_computation | async-start | bytes 8388608 | tf_op jit(solution)/shard_map/all_to_all | solution.py:172
  92.0 318.9 %all-gather.14.cloned.1.call-start = ((), (), s32[]{:S(2)}) async-start(), calls=%async_computation.6 | async-start | bytes 6684672 | tf_op jit(solution)/shard_map/all_gather | solution.py:171
  260.4 313.5 %all-gather.16.cloned.1.call-start = ((), (), s32[]{:S(2)}) async-start(), calls=%async_computation.7 | async-start | bytes 6684672 | tf_op jit(solution)/shard_map/all_gather | solution.py:171
  587.0 97.5 %all-to-all-start.3 = ((f32[16,256,256]{2,1,0:T(8,128)}), f32[16,256,256]{2,1,0:T(8,128)}, u32[]{:S(2)}, u32[]{:S(2)}) async-start(f32[16,256,256]{2,1,0:T(8,128)} %right_product.7), calls=%async_computation.3 | async-start | bytes 8388608 | tf_op jit(solution)/shard_map/all_to_all | solution.py:172
  684.5 14.9 %copy-start = (f32[32,1,128]{2,1,0:T(1,128)S(1)}, f32[32,1,128]{2,1,0:T(1,128)}, u32[]{:S(2)}) copy-start(f32[32,1,128]{2,1,0:T(1,128)} %get-tuple-element.20.mean_ref) | copy-start | bytes 49156
  684.5 14.9 %copy-start.1 = (f32[32,1,128]{2,1,0:T(1,128)S(1)}, f32[32,1,128]{2,1,0:T(1,128)}, u32[]{:S(2)}) copy-start(f32[32,1,128]{2,1,0:T(1,128)} %get-tuple-element.24.mean_ref) | copy-start | bytes 49156
  684.5 14.9 %copy-start.2 = (f32[32,1,128]{2,1,0:T(1,128)S(1)}, f32[32,1,128]{2,1,0:T(1,128)}, u32[]{:S(2)}) copy-start(f32[32,1,128]{2,1,0:T(1,128)} %get-tuple-element.27.mean_ref) | copy-start | bytes 49156
Sparse Core Ops, SparseCore 0:
  10.9 62.4 all-gather.9
  86.4 119.6 all-gather.11
  260.5 108.2 all-gather.13
  424.0 108.2 all-gather.15

commit v4 on v1

--- a/solution.py
+++ b/solution.py
@@ -42,6 +42,26 @@
     return jnp.concatenate([ref[pattern_ref[at + k]] for k in range(PER_ROW)], axis=1)
 
 
+def split_kernel(gain_ref, high_ref, low_ref):
+    high_ref[...], low_ref[...] = gain_parts(gain_ref)
+
+
+def split_gain(gain, local):
+    shape = jax.ShapeDtypeStruct((WIDTH, PER_ROW * TILE), jnp.bfloat16)
+    return pl.pallas_call(
+        split_kernel,
+        out_shape=(shape, shape),
+        grid=(STEPS,),
+        in_specs=[pl.BlockSpec((STEP // local, PER_ROW, local, TILE), lambda i: (i, 0, 0, 0))],
+        out_specs=[pl.BlockSpec((STEP, PER_ROW * TILE), lambda i: (i, 0))] * 2,
+        compiler_params=pltpu.CompilerParams(vmem_limit_bytes=VMEM),
+        cost_estimate=pl.CostEstimate(
+            flops=3 * gain.size, bytes_accessed=8 * gain.size, transcendentals=0
+        ),
+        name="split_gain",
+    )(gain)
+
+
 def right_kernel(block, pattern_ref, cov_ref, gain_ref, send_ref, high, low):
     step = pl.program_id(0)
 
@@ -61,7 +81,7 @@
     send_ref[...] = jnp.concatenate(rows, axis=0).reshape(STEP // local, local, local)
 
 
-def left_kernel(block, pattern_ref, recv_ref, gain_ref, noise_ref, mean_ref, offset_ref, *rest):
+def left_kernel(block, pattern_ref, recv_ref, gh_ref, gl_ref, noise_ref, mean_ref, offset_ref, *rest):
     cov_ref, new_mean_ref, high, low = rest[-4:]
     step = pl.program_id(0)
     local = recv_ref.shape[1]
@@ -79,12 +99,11 @@
             m = jnp.broadcast_to(mean_ref[p], (PAD, TILE))
             high[p, local:], low[p, local:] = split(m)
 
-    gh, gl = gain_parts(gain_ref)
     for i in range(STEP // TILE):
         tile = step * (STEP // TILE) + i
         xh, xl = picked(high, pattern_ref, block, tile), picked(low, pattern_ref, block, tile)
         s = slice(i * TILE, (i + 1) * TILE)
-        out = product(xh, xl, gh[s], gl[s])
+        out = product(xh, xl, gh_ref[s], gl_ref[s])
         cov_ref[:, s] = out[:local] + noise_ref[:, s]
         new_mean_ref[i] = out[local:local + 1] + offset_ref[i]
 
@@ -113,22 +132,22 @@
     )(pattern, cov, gain)
 
 
-def left(block, pattern, recv, gain, noise, mean, offset, stack, n, local):
-    per = STEP // local
+def left(block, pattern, recv, gain_high, gain_low, noise, mean, offset, stack, n, local):
     tiles = STEP // TILE
     in_specs = [
         pl.BlockSpec((n, local, local), lambda i, s: (0, 0, 0)),
-        pl.BlockSpec((per, PER_ROW, local, TILE), lambda i, s: (i, 0, 0, 0)),
+        pl.BlockSpec((STEP, PER_ROW * TILE), lambda i, s: (i, 0)),
+        pl.BlockSpec((STEP, PER_ROW * TILE), lambda i, s: (i, 0)),
         pl.BlockSpec((None, local, STEP), lambda i, s: (block, 0, i)),
         pl.BlockSpec((TILE_ROWS, 1, TILE), lambda i, s: (0, 0, 0)),
         pl.BlockSpec((tiles, 1, TILE), lambda i, s: (i, 0, 0)),
     ]
-    args = [pattern, recv, gain, noise, mean, offset]
+    args = [pattern, recv, gain_high, gain_low, noise, mean, offset]
     aliases = {}
     if stack is not None:
         in_specs.append(pl.BlockSpec(memory_space=pl.ANY))
         args.append(stack)
-        aliases = {6: 0}
+        aliases = {7: 0}
     return pl.pallas_call(
         functools.partial(left_kernel, block),
         out_shape=(
@@ -166,9 +185,11 @@
             send = right(b, pattern, last_covariance, None, gathered[b], n, local)
         else:
             send = right(b, pattern, stack, b + 1, gathered[b], n, local)
+        send, gain = lax.optimization_barrier((send, gathered[b]))
+        high, low = split_gain(gain, local)
         recv = lax.all_to_all(send, "rows", split_axis=0, concat_axis=0, tiled=True)
         stack, mean = left(
-            b, pattern, recv, gathered[b], noise_covariance, mean, vectors[b], stack, n, local
+            b, pattern, recv, high, low, noise_covariance, mean, vectors[b], stack, n, local
         )
         means[b] = mean.reshape(WIDTH)
     first = lax.axis_index("rows") * local

time: 675 us -> 683 us (1.012)
  blocking collectives: 238 us -> 141 us
  waiting for transfers between devices: 286 us -> 355 us
  Pallas kernels: 111 us -> 142 us
    all_to_all x1 -> x0, blocking collectives: 96.9 us -> none  [shards(): recv = lax.all_to_all(send, 'rows', split_axis=0, concat_axis=0, tiled=True)]
    all_to_all x3 -> x4, waiting for transfers between devices: 223 us -> 292 us  [shards(): recv = lax.all_to_all(send, 'rows', split_axis=0, concat_axis=0, tiled=True)]
    pallas_call x0 -> x4, Pallas kernels: none -> 31.3 us  [split_gain(): pl.pallas_call(split_kernel, out_shape=(shape, shape), grid=(STEPS,), in_...]
    all_to_all x3 -> x4, starting transfers between devices: 17.6 us -> 22.2 us  [shards(): recv = lax.all_to_all(send, 'rows', split_axis=0, concat_axis=0, tiled=True)]
  transfers between devices with their start and end apart: 7 -> 8, of which waited for: 3 -> 4; matrix products, arithmetic and copies ran while one was open for 0% -> 0% of each run, Pallas kernels for 12% -> 17%
where the time goes in v4:
time: 683 us; the launch traced here: 680 us
  waiting for transfers between devices  355 us (52%)
  Pallas kernels  142 us (21%)
  blocking collectives  141 us (21%)
  starting transfers between devices  22.4 us (3%)
  between operations  13.8 us (2%)
    all_to_all x4, waiting for transfers between devices, shards(): recv = lax.all_to_all(send, 'rows', split_axis=0, concat_axis=0, tiled=True)  292 us
    all_gather x1, blocking collectives, shards(): lax.all_gather(jnp.concatenate([offset_terms, last_mean[None]], 0), 'rows')  141 us
    all_gather x4, waiting for transfers between devices, shards(): lax.all_gather(gains[b], 'rows')  61.3 us
    pallas_call x4, Pallas kernels, left(): pl.pallas_call(functools.partial(left_kernel, block), out_shape=(jax.Shap...  58.5 us
    pallas_call x4, Pallas kernels, right(): pl.pallas_call(functools.partial(right_kernel, block), out_shape=jax.Shap...  51.9 us
    pallas_call x4, Pallas kernels, split_gain(): pl.pallas_call(split_kernel, out_shape=(shape, shape), grid=(STEPS,), in_...  31.3 us
    all_to_all x4, starting transfers between devices, shards(): recv = lax.all_to_all(send, 'rows', split_axis=0, concat_axis=0, tiled=True)  22.2 us
  transfers between devices with their start and end apart: 8, of which 4 were waited for; matrix products, arithmetic and copies ran while one was open for 0% of the time, Pallas kernels for 17%

profile of v4, /device:TPU:13, one launch (start us, length us, event | category | flops | bytes accessed | tf_op | source)
XLA Modules:
  0.0 680.1 jit_solution(15229890435204309670)
XLA Ops:
  7.2 0.0 all-gather.7.cloned.1.call-start
  7.2 2.5 fusion.3
  9.7 0.0 all-gather.7.cloned.1.call-update
  9.7 0.0 all-gather.9.cloned.1.call-start
  9.8 0.7 all-gather.9.cloned.1.call-update
  10.5 0.8 copy.12
  11.3 0.8 reshape.18.pattern_ref
  12.1 61.3 %all-gather.7.cloned.1.call-done.gain_ref = f32[16,3,256,128]{3,2,1,0:T(8,128)} async-done(((f32[1,3,256,128]{3,2,1,0:T(8,128)}), f32[16,3,256,128]{3,2,1,0:T(8,128)}) %all-gather.7.cloned.1.call-update) | async-done | bytes 6291472 | tf_op jit(solution)/shard_map/all_gather | solution.py:177
  73.3 13.0 %right_product.4 = f32[16,256,256]{2,1,0:T(8,128)} custom-call(s32[384]{0:T(512)} %reshape.18.pattern_ref, f32[256,4096]{1,0:T(8,128)} %cov_ref.1, f32[16,3,256,128]{3,2,1,0:T(8,128)} %all-gather.7.cloned.1.call-done.gain_ref), custom_call_target="tpu_custom_call" | custom-call | tf_op jit(solution)/shard_map/right_product/pallas_call | solution.py:117
  86.3 0.0 copy-start.3
  86.3 0.0 copy-start.4
  86.3 5.8 all-to-all-start
  92.1 0.0 all-gather.11.cloned.1.call-start
  92.2 0.7 all-gather.11.cloned.1.call-update
  92.8 0.0 copy-done.3
  92.9 0.0 copy-done.4
  92.9 141.1 %all-gather.1 = f32[16,5,256]{2,1,0:T(8,128)S(1)} all-gather(f32[1,5,256]{2,1,0:T(8,128)S(1)} %maximum_bitcast_fusion), channel_id=2, replica_groups=mesh['parts'=2,'rows'=16] {'rows'}, dimensions={0}, use_global_device_ids=true | all-gather | bytes 87040 | tf_op jit(solution)/shard_map/all_gather | solution.py:178
  234.0 0.7 fusion.4
  234.7 7.8 %split_gain.4 = (bf16[4096,384]{1,0:T(8,128)(2,1)}, bf16[4096,384]{1,0:T(8,128)(2,1)}) custom-call(f32[16,3,256,128]{3,2,1,0:T(8,128)} %all-gather.7.cloned.1.call-done.gain_ref), custom_call_target="tpu_custom_call" | custom-call | flops 4718592 | bytes 12582912 | tf_op jit(solution)/shard_map/split_gain/pallas_call | solution.py:51
  242.5 0.0 all-to-all-done.recv_ref
  242.5 14.6 %left_product.4 = (f32[4,256,4096]{2,1,0:T(8,128)}, f32[32,1,128]{2,1,0:T(1,128)}) custom-call(s32[384]{0:T(512)} %reshape.18.pattern_ref, f32[16,256,256]{2,1,0:T(8,128)} %all-to-all-done.recv_ref, bf16[4096,384]{1,0:T(8,128)(2,1)} %get-tuple-element.28.gh_ref, bf16[4096,384]{1,0:T(8,128)(2,1)} %get-tuple-element.29.gl_ref, f32[4,256,4096]{2,1,0:T(8,128)} %noise_ref.7, ...), custom_call_target="tpu_custom_call" | custom-call | tf_op jit(solution)/shard_map/left_product/pallas_call | solution.py:151
  257.1 0.0 all-gather.9.cloned.1.call-done.gain_ref
  257.2 13.0 %right_product.5 = f32[16,256,256]{2,1,0:T(8,128)} custom-call(s32[384]{0:T(512)} %reshape.18.pattern_ref, f32[4,256,4096]{2,1,0:T(8,128)} %get-tuple-element.30.cov_ref.rest_0_, f32[16,3,256,128]{3,2,1,0:T(8,128)} %all-gather.9.cloned.1.call-done.gain_ref), custom_call_target="tpu_custom_call" | custom-call | tf_op jit(solution)/shard_map/right_product/pallas_call | solution.py:117
  270.2 7.0 %all-to-all-start.1 = ((f32[16,256,256]{2,1,0:T(8,128)}), f32[16,256,256]{2,1,0:T(8,128)}, u32[]{:S(2)}, u32[]{:S(2)}) async-start(f32[16,256,256]{2,1,0:T(8,128)} %right_product.5), calls=%async_computation.1 | async-start | bytes 8388608 | tf_op jit(solution)/shard_map/all_to_all | solution.py:190
  277.2 0.0 all-gather.13.cloned.1.call-start
  277.2 0.5 all-gather.13.cloned.1.call-update
  277.8 7.8 %split_gain.5 = (bf16[4096,384]{1,0:T(8,128)(2,1)}, bf16[4096,384]{1,0:T(8,128)(2,1)}) custom-call(f32[16,3,256,128]{3,2,1,0:T(8,128)} %all-gather.9.cloned.1.call-done.gain_ref), custom_call_target="tpu_custom_call" | custom-call | flops 4718592 | bytes 12582912 | tf_op jit(solution)/shard_map/split_gain/pallas_call | solution.py:51
  285.6 122.4 %all-to-all-done.1.recv_ref = f32[16,256,256]{2,1,0:T(8,128)} async-done(((f32[16,256,256]{2,1,0:T(8,128)}), f32[16,256,256]{2,1,0:T(8,128)}, u32[]{:S(2)}, u32[]{:S(2)}) %all-to-all-start.1) | async-done | bytes 4194336 | tf_op jit(solution)/shard_map/all_to_all | solution.py:190
  408.0 14.6 %left_product.5 = (f32[4,256,4096]{2,1,0:T(8,128)}, f32[32,1,128]{2,1,0:T(1,128)}) custom-call(s32[384]{0:T(512)} %reshape.18.pattern_ref, f32[16,256,256]{2,1,0:T(8,128)} %all-to-all-done.1.recv_ref, bf16[4096,384]{1,0:T(8,128)(2,1)} %get-tuple-element.33.gh_ref, bf16[4096,384]{1,0:T(8,128)(2,1)} %get-tuple-element.34.gl_ref, ...), custom_call_target="tpu_custom_call", output_to_operand_aliasing={{0}: (7, {})} | custom-call | tf_op jit(solution)/shard_map/left_product/pallas_call | solution.py:151
  422.6 0.0 all-gather.11.cloned.1.call-done.gain_ref
  422.6 12.9 %right_product.6 = f32[16,256,256]{2,1,0:T(8,128)} custom-call(s32[384]{0:T(512)} %reshape.18.pattern_ref, f32[4,256,4096]{2,1,0:T(8,128)} %get-tuple-element.36.cov_ref.rest_0_, f32[16,3,256,128]{3,2,1,0:T(8,128)} %all-gather.11.cloned.1.call-done.gain_ref), custom_call_target="tpu_custom_call" | custom-call | tf_op jit(solution)/shard_map/right_product/pallas_call | solution.py:117
  435.5 4.5 all-to-all-start.2
  440.0 7.8 %split_gain.6 = (bf16[4096,384]{1,0:T(8,128)(2,1)}, bf16[4096,384]{1,0:T(8,128)(2,1)}) custom-call(f32[16,3,256,128]{3,2,1,0:T(8,128)} %all-gather.11.cloned.1.call-done.gain_ref), custom_call_target="tpu_custom_call" | custom-call | flops 4718592 | bytes 12582912 | tf_op jit(solution)/shard_map/split_gain/pallas_call | solution.py:51
  447.9 84.6 %all-to-all-done.2.recv_ref = f32[16,256,256]{2,1,0:T(8,128)} async-done(((f32[16,256,256]{2,1,0:T(8,128)}), f32[16,256,256]{2,1,0:T(8,128)}, u32[]{:S(2)}, u32[]{:S(2)}) %all-to-all-start.2) | async-done | bytes 4194336 | tf_op jit(solution)/shard_map/all_to_all | solution.py:190
  532.5 14.6 %left_product.6 = (f32[4,256,4096]{2,1,0:T(8,128)}, f32[32,1,128]{2,1,0:T(1,128)}) custom-call(s32[384]{0:T(512)} %reshape.18.pattern_ref, f32[16,256,256]{2,1,0:T(8,128)} %all-to-all-done.2.recv_ref, bf16[4096,384]{1,0:T(8,128)(2,1)} %get-tuple-element.39.gh_ref, bf16[4096,384]{1,0:T(8,128)(2,1)} %get-tuple-element.40.gl_ref, ...), custom_call_target="tpu_custom_call", output_to_operand_aliasing={{0}: (7, {})} | custom-call | tf_op jit(solution)/shard_map/left_product/pallas_call | solution.py:151
  547.1 0.0 all-gather.13.cloned.1.call-done.gain_ref
  547.1 13.0 %right_product.7 = f32[16,256,256]{2,1,0:T(8,128)} custom-call(s32[384]{0:T(512)} %reshape.18.pattern_ref, f32[4,256,4096]{2,1,0:T(8,128)} %get-tuple-element.42.cov_ref.rest_0_, f32[16,3,256,128]{3,2,1,0:T(8,128)} %all-gather.13.cloned.1.call-done.gain_ref), custom_call_target="tpu_custom_call" | custom-call | tf_op jit(solution)/shard_map/right_product/pallas_call | solution.py:117
  560.1 4.9 all-to-all-start.3
  565.0 7.8 %split_gain.7 = (bf16[4096,384]{1,0:T(8,128)(2,1)}, bf16[4096,384]{1,0:T(8,128)(2,1)}) custom-call(f32[16,3,256,128]{3,2,1,0:T(8,128)} %all-gather.13.cloned.1.call-done.gain_ref), custom_call_target="tpu_custom_call" | custom-call | flops 4718592 | bytes 12582912 | tf_op jit(solution)/shard_map/split_gain/pallas_call | solution.py:51
  572.9 84.6 %all-to-all-done.3.recv_ref = f32[16,256,256]{2,1,0:T(8,128)} async-done(((f32[16,256,256]{2,1,0:T(8,128)}), f32[16,256,256]{2,1,0:T(8,128)}, u32[]{:S(2)}, u32[]{:S(2)}) %all-to-all-start.3) | async-done | bytes 4194336 | tf_op jit(solution)/shard_map/all_to_all | solution.py:190
  657.5 0.0 copy-start
  657.5 0.0 copy-start.1
  657.5 0.0 copy-start.2
  657.5 14.7 %left_product.7 = (f32[4,256,4096]{2,1,0:T(8,128)}, f32[32,1,128]{2,1,0:T(1,128)}) custom-call(s32[384]{0:T(512)} %reshape.18.pattern_ref, f32[16,256,256]{2,1,0:T(8,128)} %all-to-all-done.3.recv_ref, bf16[4096,384]{1,0:T(8,128)(2,1)} %get-tuple-element.45.gh_ref, bf16[4096,384]{1,0:T(8,128)(2,1)} %get-tuple-element.46.gl_ref, ...), custom_call_target="tpu_custom_call", output_to_operand_aliasing={{0}: (7, {})} | custom-call | tf_op jit(solution)/shard_map/left_product/pallas_call | solution.py:151
  672.2 0.0 copy-done
  672.2 0.0 copy-done.1
  672.3 0.0 copy-done.2
  672.3 1.3 fusion.2
  (1 shorter events, 0.0 us)
Async XLA Ops:
  7.2 66.2 %all-gather.7.cloned.1.call-start = ((), (), s32[]{:S(2)}) async-start(), calls=%async_computation.4 | async-start | bytes 6684672 | tf_op jit(solution)/shard_map/all_gather | solution.py:177
  9.7 247.4 %all-gather.9.cloned.1.call-start = ((), (), s32[]{:S(2)}) async-start(), calls=%async_computation.5 | async-start | bytes 6684672 | tf_op jit(solution)/shard_map/all_gather | solution.py:177
  86.3 6.6 copy-start.3
  86.3 6.6 copy-start.4
  86.3 156.2 %all-to-all-start = ((f32[16,256,256]{2,1,0:T(8,128)}), f32[16,256,256]{2,1,0:T(8,128)}, u32[]{:S(2)}, u32[]{:S(2)}) async-start(f32[16,256,256]{2,1,0:T(8,128)} %right_product.4), calls=%async_computation | async-start | bytes 8388608 | tf_op jit(solution)/shard_map/all_to_all | solution.py:190
  92.1 330.5 %all-gather.11.cloned.1.call-start = ((), (), s32[]{:S(2)}) async-start(), calls=%async_computation.6 | async-start | bytes 6684672 | tf_op jit(solution)/shard_map/all_gather | solution.py:177
  270.2 137.8 %all-to-all-start.1 = ((f32[16,256,256]{2,1,0:T(8,128)}), f32[16,256,256]{2,1,0:T(8,128)}, u32[]{:S(2)}, u32[]{:S(2)}) async-start(f32[16,256,256]{2,1,0:T(8,128)} %right_product.5), calls=%async_computation.1 | async-start | bytes 8388608 | tf_op jit(solution)/shard_map/all_to_all | solution.py:190
  277.2 269.9 %all-gather.13.cloned.1.call-start = ((), (), s32[]{:S(2)}) async-start(), calls=%async_computation.7 | async-start | bytes 6684672 | tf_op jit(solution)/shard_map/all_gather | solution.py:177
  435.5 97.0 %all-to-all-start.2 = ((f32[16,256,256]{2,1,0:T(8,128)}), f32[16,256,256]{2,1,0:T(8,128)}, u32[]{:S(2)}, u32[]{:S(2)}) async-start(f32[16,256,256]{2,1,0:T(8,128)} %right_product.6), calls=%async_computation.2 | async-start | bytes 8388608 | tf_op jit(solution)/shard_map/all_to_all | solution.py:190
  560.1 97.4 %all-to-all-start.3 = ((f32[16,256,256]{2,1,0:T(8,128)}), f32[16,256,256]{2,1,0:T(8,128)}, u32[]{:S(2)}, u32[]{:S(2)}) async-start(f32[16,256,256]{2,1,0:T(8,128)} %right_product.7), calls=%async_computation.3 | async-start | bytes 8388608 | tf_op jit(solution)/shard_map/all_to_all | solution.py:190
  657.5 14.7 %copy-start = (f32[32,1,128]{2,1,0:T(1,128)S(1)}, f32[32,1,128]{2,1,0:T(1,128)}, u32[]{:S(2)}) copy-start(f32[32,1,128]{2,1,0:T(1,128)} %get-tuple-element.35.mean_ref) | copy-start | bytes 49156
  657.5 14.7 %copy-start.1 = (f32[32,1,128]{2,1,0:T(1,128)S(1)}, f32[32,1,128]{2,1,0:T(1,128)}, u32[]{:S(2)}) copy-start(f32[32,1,128]{2,1,0:T(1,128)} %get-tuple-element.41.mean_ref) | copy-start | bytes 49156
  657.5 14.7 %copy-start.2 = (f32[32,1,128]{2,1,0:T(1,128)S(1)}, f32[32,1,128]{2,1,0:T(1,128)}, u32[]{:S(2)}) copy-start(f32[32,1,128]{2,1,0:T(1,128)} %get-tuple-element.47.mean_ref) | copy-start | bytes 49156
Sparse Core Ops, SparseCore 0:
  10.9 62.4 all-gather.6
  75.6 115.3 all-gather.8
  193.3 70.6 all-gather.10
  280.0 110.6 all-gather.12

commit v5 on v1

--- a/solution.py
+++ b/solution.py
@@ -29,7 +29,7 @@
 
 
 def product(ah, al, bh, bl):
-    return nt(ah, bh) + (nt(ah, bl) + nt(al, bh))
+    return nt(jnp.concatenate([ah, ah, al], axis=1), jnp.concatenate([bh, bl, bh], axis=1))
 
 
 def gain_parts(gain_ref):

time: 675 us -> 673 us (level)
  no operation moved by 1% of the time
where the time goes in v5:
time: 673 us; the launch traced here: 671 us
  waiting for transfers between devices  286 us (42%)
  blocking collectives  238 us (35%)
  Pallas kernels  109 us (16%)
  starting transfers between devices  17.9 us (3%)
  between operations  13.8 us (2%)
    all_to_all x3, waiting for transfers between devices, shards(): recv = lax.all_to_all(send, 'rows', split_axis=0, concat_axis=0, tiled=True)  222 us
    all_gather x1, blocking collectives, shards(): lax.all_gather(jnp.concatenate([offset_terms, last_mean[None]], 0), 'rows')  141 us
    all_to_all x1, blocking collectives, shards(): recv = lax.all_to_all(send, 'rows', split_axis=0, concat_axis=0, tiled=True)  97.1 us
    all_gather x4, waiting for transfers between devices, shards(): lax.all_gather(gains[b], 'rows')  61.3 us
    pallas_call x4, Pallas kernels, left(): pl.pallas_call(functools.partial(left_kernel, block), out_shape=(jax.Shap...  56.5 us
    pallas_call x4, Pallas kernels, right(): pl.pallas_call(functools.partial(right_kernel, block), out_shape=jax.Shap...  52.8 us
    all_to_all x3, starting transfers between devices, shards(): recv = lax.all_to_all(send, 'rows', split_axis=0, concat_axis=0, tiled=True)  17.7 us
  transfers between devices with their start and end apart: 7, of which 3 were waited for; matrix products, arithmetic and copies ran while one was open for 0% of the time, Pallas kernels for 12%

profile of v5, /device:TPU:13, one launch (start us, length us, event | category | flops | bytes accessed | tf_op | source)
XLA Modules:
  0.0 670.9 jit_solution(2994689564894816690)
XLA Ops:
  7.2 0.0 all-gather.7.cloned.1.call-start
  7.2 2.5 fusion.3
  9.7 0.0 all-gather.7.cloned.1.call-update
  9.7 0.0 all-gather.9.cloned.1.call-start
  9.8 0.7 all-gather.9.cloned.1.call-update
  10.5 0.8 copy.12
  11.3 0.8 reshape.18.pattern_ref
  12.1 61.3 %all-gather.7.cloned.1.call-done.gain_ref = f32[16,3,256,128]{3,2,1,0:T(8,128)} async-done(((f32[1,3,256,128]{3,2,1,0:T(8,128)}), f32[16,3,256,128]{3,2,1,0:T(8,128)}) %all-gather.7.cloned.1.call-update) | async-done | bytes 6291472 | tf_op jit(solution)/shard_map/all_gather | solution.py:158
  73.3 13.1 %right_product.4 = f32[16,256,256]{2,1,0:T(8,128)} custom-call(s32[384]{0:T(512)} %reshape.18.pattern_ref, f32[256,4096]{1,0:T(8,128)} %cov_ref.1, f32[16,3,256,128]{3,2,1,0:T(8,128)} %all-gather.7.cloned.1.call-done.gain_ref), custom_call_target="tpu_custom_call" | custom-call | tf_op jit(solution)/shard_map/right_product/pallas_call | solution.py:98
  86.5 0.0 copy-start.3
  86.5 0.0 copy-start.4
  86.5 5.8 all-to-all-start
  92.3 0.0 all-gather.11.cloned.1.call-start
  92.3 0.7 all-gather.11.cloned.1.call-update
  93.0 0.0 copy-done.3
  93.0 0.0 copy-done.4
  93.1 141.2 %all-gather.1 = f32[16,5,256]{2,1,0:T(8,128)S(1)} all-gather(f32[1,5,256]{2,1,0:T(8,128)S(1)} %maximum_bitcast_fusion), channel_id=2, replica_groups=mesh['parts'=2,'rows'=16] {'rows'}, dimensions={0}, use_global_device_ids=true | all-gather | bytes 87040 | tf_op jit(solution)/shard_map/all_gather | solution.py:159
  234.2 0.7 fusion.4
  234.9 0.0 all-to-all-done.recv_ref
  234.9 14.1 %left_product.4 = (f32[4,256,4096]{2,1,0:T(8,128)}, f32[32,1,128]{2,1,0:T(1,128)}) custom-call(s32[384]{0:T(512)} %reshape.18.pattern_ref, f32[16,256,256]{2,1,0:T(8,128)} %all-to-all-done.recv_ref, f32[16,3,256,128]{3,2,1,0:T(8,128)} %all-gather.7.cloned.1.call-done.gain_ref, f32[4,256,4096]{2,1,0:T(8,128)} %noise_ref.7, f32[32,1,128]{2,1,0:T(1,128)} %bitcast.23, ...), custom_call_target="tpu_custom_call" | custom-call | tf_op jit(solution)/shard_map/left_product/pallas_call | solution.py:132
  249.1 0.0 all-gather.9.cloned.1.call-done.gain_ref
  249.1 13.4 %right_product.5 = f32[16,256,256]{2,1,0:T(8,128)} custom-call(s32[384]{0:T(512)} %reshape.18.pattern_ref, f32[4,256,4096]{2,1,0:T(8,128)} %get-tuple-element.10.cov_ref.rest_0_, f32[16,3,256,128]{3,2,1,0:T(8,128)} %all-gather.9.cloned.1.call-done.gain_ref), custom_call_target="tpu_custom_call" | custom-call | tf_op jit(solution)/shard_map/right_product/pallas_call | solution.py:98
  262.5 6.6 all-to-all-start.1
  269.1 0.0 all-gather.13.cloned.1.call-start
  269.1 0.5 all-gather.13.cloned.1.call-update
  269.6 129.9 %all-to-all-done.1.recv_ref = f32[16,256,256]{2,1,0:T(8,128)} async-done(((f32[16,256,256]{2,1,0:T(8,128)}), f32[16,256,256]{2,1,0:T(8,128)}, u32[]{:S(2)}, u32[]{:S(2)}) %all-to-all-start.1) | async-done | bytes 4194336 | tf_op jit(solution)/shard_map/all_to_all | solution.py:169
  399.6 14.1 %left_product.5 = (f32[4,256,4096]{2,1,0:T(8,128)}, f32[32,1,128]{2,1,0:T(1,128)}) custom-call(s32[384]{0:T(512)} %reshape.18.pattern_ref, f32[16,256,256]{2,1,0:T(8,128)} %all-to-all-done.1.recv_ref, f32[16,3,256,128]{3,2,1,0:T(8,128)} %all-gather.9.cloned.1.call-done.gain_ref, f32[4,256,4096]{2,1,0:T(8,128)} %noise_ref.7, ...), custom_call_target="tpu_custom_call", output_to_operand_aliasing={{0}: (6, {})} | custom-call | tf_op jit(solution)/shard_map/left_product/pallas_call | solution.py:132
  413.7 0.0 all-gather.11.cloned.1.call-done.gain_ref
  413.7 13.1 %right_product.6 = f32[16,256,256]{2,1,0:T(8,128)} custom-call(s32[384]{0:T(512)} %reshape.18.pattern_ref, f32[4,256,4096]{2,1,0:T(8,128)} %get-tuple-element.12.cov_ref.rest_0_, f32[16,3,256,128]{3,2,1,0:T(8,128)} %all-gather.11.cloned.1.call-done.gain_ref), custom_call_target="tpu_custom_call" | custom-call | tf_op jit(solution)/shard_map/right_product/pallas_call | solution.py:98
  426.8 97.1 %all_to_all.20.recv_ref = f32[16,256,256]{2,1,0:T(8,128)} all-to-all(f32[16,256,256]{2,1,0:T(8,128)} %right_product.6), channel_id=1, replica_groups=mesh['parts'=2,'rows'=16] {'rows'}, dimensions={0} | all-to-all | bytes 8388608 | tf_op jit(solution)/shard_map/all_to_all | solution.py:169
  523.9 14.1 %left_product.6 = (f32[4,256,4096]{2,1,0:T(8,128)}, f32[32,1,128]{2,1,0:T(1,128)}) custom-call(s32[384]{0:T(512)} %reshape.18.pattern_ref, f32[16,256,256]{2,1,0:T(8,128)} %all_to_all.20.recv_ref, f32[16,3,256,128]{3,2,1,0:T(8,128)} %all-gather.11.cloned.1.call-done.gain_ref, f32[4,256,4096]{2,1,0:T(8,128)} %noise_ref.7, ...), custom_call_target="tpu_custom_call", output_to_operand_aliasing={{0}: (6, {})} | custom-call | tf_op jit(solution)/shard_map/left_product/pallas_call | solution.py:132
  538.0 0.0 all-gather.13.cloned.1.call-done.gain_ref
  538.0 13.1 %right_product.7 = f32[16,256,256]{2,1,0:T(8,128)} custom-call(s32[384]{0:T(512)} %reshape.18.pattern_ref, f32[4,256,4096]{2,1,0:T(8,128)} %get-tuple-element.14.cov_ref.rest_0_, f32[16,3,256,128]{3,2,1,0:T(8,128)} %all-gather.13.cloned.1.call-done.gain_ref), custom_call_target="tpu_custom_call" | custom-call | tf_op jit(solution)/shard_map/right_product/pallas_call | solution.py:98
  551.1 5.3 all-to-all-start.3
  556.4 92.5 %all-to-all-done.3.recv_ref = f32[16,256,256]{2,1,0:T(8,128)} async-done(((f32[16,256,256]{2,1,0:T(8,128)}), f32[16,256,256]{2,1,0:T(8,128)}, u32[]{:S(2)}, u32[]{:S(2)}) %all-to-all-start.3) | async-done | bytes 4194336 | tf_op jit(solution)/shard_map/all_to_all | solution.py:169
  648.8 0.0 copy-start
  648.8 0.0 copy-start.1
  648.8 0.0 copy-start.2
  648.8 14.2 %left_product.7 = (f32[4,256,4096]{2,1,0:T(8,128)}, f32[32,1,128]{2,1,0:T(1,128)}) custom-call(s32[384]{0:T(512)} %reshape.18.pattern_ref, f32[16,256,256]{2,1,0:T(8,128)} %all-to-all-done.3.recv_ref, f32[16,3,256,128]{3,2,1,0:T(8,128)} %all-gather.13.cloned.1.call-done.gain_ref, f32[4,256,4096]{2,1,0:T(8,128)} %noise_ref.7, ...), custom_call_target="tpu_custom_call", output_to_operand_aliasing={{0}: (6, {})} | custom-call | tf_op jit(solution)/shard_map/left_product/pallas_call | solution.py:132
  663.1 0.0 copy-done
  663.1 0.0 copy-done.1
  663.1 0.0 copy-done.2
  663.1 1.3 fusion.2
  (1 shorter events, 0.0 us)
Async XLA Ops:
  7.2 66.2 %all-gather.7.cloned.1.call-start = ((), (), s32[]{:S(2)}) async-start(), calls=%async_computation.4 | async-start | bytes 6684672 | tf_op jit(solution)/shard_map/all_gather | solution.py:158
  9.7 239.3 %all-gather.9.cloned.1.call-start = ((), (), s32[]{:S(2)}) async-start(), calls=%async_computation.5 | async-start | bytes 6684672 | tf_op jit(solution)/shard_map/all_gather | solution.py:158
  86.5 6.6 copy-start.3
  86.5 6.6 copy-start.4
  86.5 148.4 %all-to-all-start = ((f32[16,256,256]{2,1,0:T(8,128)}), f32[16,256,256]{2,1,0:T(8,128)}, u32[]{:S(2)}, u32[]{:S(2)}) async-start(f32[16,256,256]{2,1,0:T(8,128)} %right_product.4), calls=%async_computation | async-start | bytes 8388608 | tf_op jit(solution)/shard_map/all_to_all | solution.py:169
  92.3 321.4 %all-gather.11.cloned.1.call-start = ((), (), s32[]{:S(2)}) async-start(), calls=%async_computation.6 | async-start | bytes 6684672 | tf_op jit(solution)/shard_map/all_gather | solution.py:158
  262.5 137.1 %all-to-all-start.1 = ((f32[16,256,256]{2,1,0:T(8,128)}), f32[16,256,256]{2,1,0:T(8,128)}, u32[]{:S(2)}, u32[]{:S(2)}) async-start(f32[16,256,256]{2,1,0:T(8,128)} %right_product.5), calls=%async_computation.1 | async-start | bytes 8388608 | tf_op jit(solution)/shard_map/all_to_all | solution.py:169
  269.1 268.9 %all-gather.13.cloned.1.call-start = ((), (), s32[]{:S(2)}) async-start(), calls=%async_computation.7 | async-start | bytes 6684672 | tf_op jit(solution)/shard_map/all_gather | solution.py:158
  551.1 97.8 %all-to-all-start.3 = ((f32[16,256,256]{2,1,0:T(8,128)}), f32[16,256,256]{2,1,0:T(8,128)}, u32[]{:S(2)}, u32[]{:S(2)}) async-start(f32[16,256,256]{2,1,0:T(8,128)} %right_product.7), calls=%async_computation.3 | async-start | bytes 8388608 | tf_op jit(solution)/shard_map/all_to_all | solution.py:169
  648.8 14.2 %copy-start = (f32[32,1,128]{2,1,0:T(1,128)S(1)}, f32[32,1,128]{2,1,0:T(1,128)}, u32[]{:S(2)}) copy-start(f32[32,1,128]{2,1,0:T(1,128)} %get-tuple-element.11.mean_ref) | copy-start | bytes 49156
  648.8 14.2 %copy-start.1 = (f32[32,1,128]{2,1,0:T(1,128)S(1)}, f32[32,1,128]{2,1,0:T(1,128)}, u32[]{:S(2)}) copy-start(f32[32,1,128]{2,1,0:T(1,128)} %get-tuple-element.13.mean_ref) | copy-start | bytes 49156
  648.8 14.2 %copy-start.2 = (f32[32,1,128]{2,1,0:T(1,128)S(1)}, f32[32,1,128]{2,1,0:T(1,128)}, u32[]{:S(2)}) copy-start(f32[32,1,128]{2,1,0:T(1,128)} %get-tuple-element.15.mean_ref) | copy-start | bytes 49156
Sparse Core Ops, SparseCore 0:
  10.9 62.4 all-gather.6
  75.6 115.3 all-gather.8
  193.3 70.6 all-gather.10
  271.9 110.6 all-gather.12
